TPU v7x, 512 devices: a whole 4x8x8 slice. The times are simulated.
512 devices in a mesh: gx: 64 (over z, x, core), gy: 8 (over y).
Axes of the slice: x: 4, y: 8, z: 8, core: 2. Of those that a mesh axis runs over, the one named last changes fastest.
Arguments:
- velocity: float32 [3, 256, 128, 256], P(None, 'gx', 'gy'), may hold values from -6 to 6
- owner_brick: int32 [65536], P(('gx', 'gy')), may hold values from 0 to 255
- particle_flags: int32 [65536], P(('gx', 'gy')), may hold values from 0 to 2, as said below
- weights: float32 [65536, 128], P(('gx', 'gy')), may hold values from 0 to 0.03125
- target_velocity: float32 [3, 65536], P(None, ('gx', 'gy')), may hold values from -6 to 6
- contact_force: float32 [3, 65536], P(None, ('gx', 'gy')), may hold values from -60 to 60
Outputs:
- velocity_new: float32 [3, 256, 128, 256], P(None, 'gx', 'gy')
- pressure_potential: float32 [256, 128, 256], P('gx', 'gy')
- particle_impulse: float32 [3, 65536], P(None, ('gx', 'gy'))
Inputs may be any that keep to these rules, and one draw needn't show every extreme that they name: `particle_flags`: 0 marks an empty slot, 1 a particle whose support is its owner brick, 2 one whose support also covers its next brick; at least 32 slots of each device are live, and on some device all 128 are.
All inputs are finite; a program needn't handle non-finite values.
Results may differ from a plain program's by a relative error of at most 0.0003.
Values sent between devices are 32-bit elements; how exact they have to be, the bound alone decides.
A program may use at most 64 MiB of HBM per device.

v0:
```python
import jax
import jax.numpy as jnp
import ml_dtypes
import numpy as np
from jax import lax
from jax.experimental import pallas as pl
from jax.experimental.pallas import tpu as pltpu
from jax.sharding import PartitionSpec as P

time_step = 0.05
viscosity = 2.0
volume_ratio = 16.0


def padded_2(cells, sides, width):
    for axis, dim in sides:
        count = lax.axis_size(axis)
        head = lax.slice_in_dim(cells, 0, width, axis=dim)
        tail = lax.slice_in_dim(cells, cells.shape[dim] - width, cells.shape[dim], axis=dim)
        cells = jnp.concatenate(
            [
                lax.ppermute(tail, axis, [(i, (i + 1) % count) for i in range(count)]),
                cells,
                lax.ppermute(head, axis, [((i + 1) % count, i) for i in range(count)]),
            ],
            axis=dim,
        )
    return cells


def shifted(array, axis, by):
    devices = lax.axis_size(axis)
    return lax.ppermute(array, axis, [(i, (i + by) % devices) for i in range(devices)])


def to_bricks(grid_field):
    components, size_x, size_y, size_z = grid_field.shape
    blocks = grid_field.reshape(components, size_x // 4, 4, size_y // 4, 4, size_z // 4, 4)
    blocks = blocks.transpose(0, 1, 3, 5, 2, 4, 6)
    return blocks.reshape(components, size_x // 4 * (size_y // 4) * (size_z // 4), 64)


def from_bricks(blocks, size_x, size_y, size_z):
    components = blocks.shape[0]
    grid_field = blocks.reshape(components, size_x // 4, size_y // 4, size_z // 4, 4, 4, 4)
    grid_field = grid_field.transpose(0, 1, 4, 2, 5, 3, 6)
    return grid_field.reshape(components, size_x, size_y, size_z)


def spread_terms(impulse, weight):
    return (impulse.T[:, :, None] * weight[:, None, :]).reshape(weight.shape[0], 192)


MESH = pl.DeviceIdType.MESH
GX, GY = 64, 8


def cas_table(points):
    index = np.arange(points)
    angle = 2.0 * np.pi * (np.outer(index, index) % points) / points
    return (np.cos(angle) + np.sin(angle)) / np.sqrt(points)


def in_two(table):
    top = table.astype(np.float32).astype(ml_dtypes.bfloat16)
    rest = (table - top.astype(np.float64)).astype(ml_dtypes.bfloat16)
    return np.stack([top, rest])


def build_tables():
    cas_128, cas_64 = cas_table(128), cas_table(64)
    depth = np.zeros((256, 256))
    for pz in range(2):
        depth[pz::2, pz * 128 : pz * 128 + 128] = cas_128
    rows = np.zeros((2, 64, 3, 8, 32))
    for py in range(2):
        for t in range(8):
            edge = (8 * t - 1) % 64 if py else (8 * t + 8) % 64
            for xi in range(3):
                rows[py, :, xi, t, 8 * xi : 8 * xi + 8] = cas_64[:, 8 * t : 8 * t + 8]
                rows[py, :, xi, t, 24 + xi] = cas_64[:, edge]
    rows = rows.reshape(2, 192, 256)
    columns = np.zeros((2, 128, 64, 3))
    for px in range(2):
        for xi in range(3):
            columns[px, :, :, xi] = cas_128[:, (2 * np.arange(64) + xi - px) % 128]
    columns = columns.reshape(2, 128, 192)

    def both(tables):
        return np.stack([in_two(table) for table in tables])

    square_128 = np.sin(np.pi * np.arange(128) / 128) ** 2
    square_64 = np.sin(np.pi * np.arange(64) / 64) ** 2
    symbol_xz = (square_128[:, None] + square_128[None, :]).astype(np.float32)
    symbol_y = np.broadcast_to(square_64[:, None], (64, 128)).astype(np.float32)
    return (
        in_two(depth),
        in_two(depth.T),
        both(rows),
        both(rows.transpose(0, 2, 1)),
        both(columns),
        both(columns.transpose(0, 2, 1)),
        symbol_xz,
        symbol_y,
    )


def halves(values):
    top = values.astype(jnp.bfloat16)
    rest = (values - top.astype(jnp.float32)).astype(jnp.bfloat16)
    return top, rest


def dot(left, right):
    return jnp.dot(left, right, preferred_element_type=jnp.float32)


def table_times(table, values):
    top, rest = halves(values)
    return dot(table[0], top) + (dot(table[1], top) + dot(table[0], rest))


def times_table(values, table):
    top, rest = halves(values)
    return dot(top, table[0]) + (dot(rest, table[0]) + dot(top, table[1]))


def exchange_gx(s, t, source, target, own_sem, send_sem, recv_sem):
    own = pltpu.make_async_copy(source.at[pl.ds(3 * s, 3)], target.at[pl.ds(3 * s, 3)], own_sem)
    own.start()

    def send(step, carry):
        peer = lax.rem(s + step, GX)
        pltpu.make_async_remote_copy(
            src_ref=source.at[pl.ds(3 * peer, 3)],
            dst_ref=target.at[pl.ds(3 * s, 3)],
            send_sem=send_sem,
            recv_sem=recv_sem,
            device_id=(peer, t),
            device_id_type=MESH,
        ).start()
        return carry

    lax.fori_loop(1, GX, send, 0)
    own.wait()
    moved = pl.ds(0, 3 * (GX - 1))
    pltpu.make_async_copy(source.at[moved], target.at[moved], recv_sem).wait()
    pltpu.make_async_copy(source.at[moved], target.at[moved], send_sem).wait()


def exchange_gy(s, t, source, target, own_sem, send_sem, recv_sem):
    own = pltpu.make_async_copy(source.at[pl.ds(32 * t, 32)], target.at[pl.ds(32 * t, 32)], own_sem)
    own.start()

    def send(step, carry):
        peer = lax.rem(t + step, GY)
        pltpu.make_async_remote_copy(
            src_ref=source.at[pl.ds(32 * peer, 27)],
            dst_ref=target.at[pl.ds(32 * t, 27)],
            send_sem=send_sem,
            recv_sem=recv_sem,
            device_id=(s, peer),
            device_id_type=MESH,
        ).start()
        return carry

    lax.fori_loop(1, GY, send, 0)
    own.wait()
    moved = pl.ds(0, 27 * (GY - 1))
    pltpu.make_async_copy(source.at[moved], target.at[moved], recv_sem).wait()
    pltpu.make_async_copy(source.at[moved], target.at[moved], send_sem).wait()


def place_of(px, xi):
    return 2 * xi + 1 - px


def put(padded, start, size, values, stride=None):
    padded[0, pl.ds(start, size, stride)] = values[:, :128]
    padded[1, pl.ds(start, size, stride)] = values[:, 128:]


def take(padded, start, size, stride=None):
    return jnp.concatenate(
        [padded[half, pl.ds(start, size, stride)] for half in range(2)], axis=1
    )


def project_kernel(
    forced,
    depth_hbm,
    depth_back_hbm,
    rows_hbm,
    rows_back_hbm,
    columns_hbm,
    columns_back_hbm,
    symbol_xz,
    symbol_y,
    velocity_new,
    potential,
    depth,
    depth_back,
    rows,
    rows_back,
    columns,
    columns_back,
    padded,
    classes,
    line_out,
    line_in,
    y_out,
    x_in,
    x_out,
    y_in,
    line_back,
    line_home,
    table_sem,
    own_sem,
    send_sem,
    recv_sem,
):
    s = lax.axis_index("gx")
    t = lax.axis_index("gy")
    px = t // 4
    py = lax.rem(t // 2, 2)
    loads = [
        pltpu.make_async_copy(source, target, table_sem.at[number])
        for number, (source, target) in enumerate(
            (
                (depth_hbm, depth),
                (depth_back_hbm, depth_back),
                (rows_hbm.at[py], rows),
                (rows_back_hbm.at[py], rows_back),
                (columns_hbm.at[px], columns),
                (columns_back_hbm.at[px], columns_back),
            )
        )
    ]
    for load in loads:
        load.start()
    line_in[...] = jnp.zeros_like(line_in)
    barrier = pltpu.get_barrier_semaphore()

    def greet_gx(step, carry):
        pl.semaphore_signal(
            barrier, inc=1, device_id=(lax.rem(s + step, GX), t), device_id_type=MESH
        )
        return carry

    def greet_gy(step, carry):
        pl.semaphore_signal(
            barrier, inc=1, device_id=(s, lax.rem(t + step, GY)), device_id_type=MESH
        )
        return carry

    lax.fori_loop(1, GY, greet_gy, 0)
    lax.fori_loop(1, GX, greet_gx, 0)

    classes[...] = jnp.zeros_like(classes)
    row_number = lax.broadcasted_iota(jnp.int32, (16, 256), 0)
    for place in range(6):
        x = place - 1
        total = jnp.zeros((16, 256), jnp.float32)
        if 0 <= x + 1 < 4:
            total = total + forced[0, x + 1]
        if 0 <= x - 1 < 4:
            total = total - forced[0, x - 1]
        if 0 <= x < 4:
            v = forced[1, x]
            w = forced[2, x]
            upper = jnp.where(row_number == 15, 0.0, pltpu.roll(v, 15, 0))
            lower = jnp.where(row_number == 0, 0.0, pltpu.roll(v, 1, 0))
            total = total + (upper - lower)
            total = total + (pltpu.roll(w, 255, 1) - pltpu.roll(w, 1, 1))
            put(padded, 32 * place + 7, 1, 0.5 * forced[1, x, 0:1])
            put(padded, 32 * place + 24, 1, -0.5 * forced[1, x, 15:16])
        else:
            put(padded, 32 * place + 7, 1, jnp.zeros((1, 256), jnp.float32))
            put(padded, 32 * place + 24, 1, jnp.zeros((1, 256), jnp.float32))
        put(padded, 32 * place + 8, 16, 0.5 * total)
    for a in range(2):
        for b in range(2):
            base = 32 * (2 * a + b)
            for xi in range(3):
                place = 32 * place_of(a, xi)
                classes[base + 8 * xi : base + 8 * xi + 8] = take(padded, place + 8 + b, 8, 2)
                edge = place + (7 if b else 24)
                classes[base + 24 + xi : base + 25 + xi] = take(padded, edge, 1)
    loads[0].wait()
    spectrum = times_table(classes[...], depth)
    for c in range(8):
        line_out[32 * c : 32 * c + 32] = spectrum[
            32 * (c // 2) : 32 * (c // 2) + 32, 128 * (c % 2) : 128 * (c % 2) + 128
        ]
    pl.semaphore_wait(barrier, GX - 1 + GY - 1)
    exchange_gy(s, t, line_out, line_in, own_sem.at[0], send_sem.at[0], recv_sem.at[0])

    loads[2].wait()
    y_out[...] = table_times(rows, line_in[...])
    exchange_gx(s, t, y_out, x_in, own_sem.at[1], send_sem.at[1], recv_sem.at[1])

    loads[4].wait()
    loads[5].wait()
    symbol = symbol_xz[...] + symbol_y[pl.ds(s, 1)]
    positive = symbol > 0
    factor = jnp.where(positive, -1.0 / jnp.where(positive, symbol, 1.0), 0.0)
    x_out[...] = table_times(columns_back, table_times(columns, x_in[...]) * factor)
    exchange_gx(s, t, x_out, y_in, own_sem.at[2], send_sem.at[2], recv_sem.at[2])

    loads[3].wait()
    line_back[...] = table_times(rows_back, y_in[...])
    exchange_gy(s, t, line_back, line_home, own_sem.at[3], send_sem.at[3], recv_sem.at[3])

    loads[1].wait()
    home = jnp.concatenate(
        [
            jnp.concatenate(
                [line_home[64 * c : 64 * c + 32], line_home[64 * c + 32 : 64 * c + 64]], axis=1
            )
            for c in range(4)
        ],
        axis=0,
    )
    classes[...] = times_table(home, depth_back)
    for a in range(2):
        for b in range(2):
            base = 32 * (2 * a + b)
            for xi in range(3):
                place = 32 * place_of(a, xi)
                put(padded, place + 8 + b, 8, classes[base + 8 * xi : base + 8 * xi + 8], 2)
                edge = place + (7 if b else 24)
                put(padded, edge, 1, classes[base + 24 + xi : base + 25 + xi])
    for x in range(4):
        base = 32 * (x + 1)
        p = take(padded, base + 8, 16)
        potential[x] = p
        velocity_new[0, x] = forced[0, x] - 0.5 * (
            take(padded, base + 40, 16) - take(padded, base - 24, 16)
        )
        velocity_new[1, x] = forced[1, x] - 0.5 * (
            take(padded, base + 9, 16) - take(padded, base + 7, 16)
        )
        velocity_new[2, x] = forced[2, x] - 0.5 * (pltpu.roll(p, 255, 1) - pltpu.roll(p, 1, 1))


def project(forced):
    tables = build_tables()
    inside = pl.BlockSpec(memory_space=pltpu.VMEM)
    anywhere = pl.BlockSpec(memory_space=pl.ANY)
    f32, bf16 = jnp.float32, jnp.bfloat16
    return pl.pallas_call(
        project_kernel,
        out_shape=(
            jax.ShapeDtypeStruct((3, 4, 16, 256), f32),
            jax.ShapeDtypeStruct((4, 16, 256), f32),
        ),
        in_specs=[inside] + [anywhere] * 6 + [inside] * 2,
        out_specs=(inside, inside),
        scratch_shapes=[
            pltpu.VMEM((2, 256, 256), bf16),
            pltpu.VMEM((2, 256, 256), bf16),
            pltpu.VMEM((2, 192, 256), bf16),
            pltpu.VMEM((2, 256, 192), bf16),
            pltpu.VMEM((2, 128, 192), bf16),
            pltpu.VMEM((2, 192, 128), bf16),
            pltpu.VMEM((2, 192, 128), f32),
            pltpu.VMEM((128, 256), f32),
            pltpu.VMEM((256, 128), f32),
            pltpu.VMEM((256, 128), f32),
            pltpu.VMEM((192, 128), f32),
            pltpu.VMEM((192, 128), f32),
            pltpu.VMEM((192, 128), f32),
            pltpu.VMEM((192, 128), f32),
            pltpu.VMEM((256, 128), f32),
            pltpu.VMEM((256, 128), f32),
            pltpu.SemaphoreType.DMA((6,)),
            pltpu.SemaphoreType.DMA((4,)),
            pltpu.SemaphoreType.DMA((4,)),
            pltpu.SemaphoreType.DMA((4,)),
        ],
        compiler_params=pltpu.CompilerParams(collective_id=0, has_side_effects=True),
    )(forced, *[jnp.asarray(table) for table in tables])


def advance(velocity):
    padded = padded_2(velocity, (("gx", 1), ("gy", 2)), 1)
    uppers = (padded[:, 2:, 1:-1], padded[:, 1:-1, 2:], jnp.roll(velocity, -1, 3))
    lowers = (padded[:, :-2, 1:-1], padded[:, 1:-1, :-2], jnp.roll(velocity, 1, 3))
    laplace = -6.0 * velocity
    carried = jnp.zeros_like(velocity)
    for direction in range(3):
        laplace = laplace + uppers[direction] + lowers[direction]
        carried = (
            carried + velocity[direction][None] * (uppers[direction] - lowers[direction]) * 0.5
        )
    return velocity + time_step * (viscosity * laplace - carried)


def body(velocity, owner_brick, particle_flags, weights, target_velocity, contact_force):
    size_x = velocity.shape[1]
    size_y = velocity.shape[2]
    size_z = velocity.shape[3]
    velocity_star = advance(velocity)
    bricks_x = size_x // 4
    layer_size = size_y // 4 * (size_z // 4)
    total_bricks = bricks_x * layer_size
    star_bricks = to_bricks(velocity_star)
    block_x = owner_brick // layer_size
    in_layer = owner_brick % layer_size
    inside = block_x < bricks_x - 1
    live_mask = (particle_flags > 0).astype(jnp.float32)
    crossing = (particle_flags == 2).astype(jnp.float32)
    own_weight = weights[:, :64] * live_mask[:, None]
    next_weight = weights[:, 64:] * crossing[:, None]
    inner_weight = next_weight * inside.astype(jnp.float32)[:, None]
    outer_weight = next_weight - inner_weight
    inner_index = jnp.where(inside, owner_brick + layer_size, owner_brick)
    interpolated = jnp.sum(star_bricks[:, owner_brick] * own_weight[None], axis=2)
    interpolated = interpolated + jnp.sum(star_bricks[:, inner_index] * inner_weight[None], axis=2)
    from_next = shifted(star_bricks, "gx", -1)
    interpolated = interpolated + jnp.sum(from_next[:, in_layer] * outer_weight[None], axis=2)
    particle_impulse = live_mask[None] * (
        target_velocity - interpolated + time_step * contact_force
    )
    outgoing = jax.ops.segment_sum(
        spread_terms(particle_impulse, outer_weight), in_layer, num_segments=layer_size
    )
    received = shifted(outgoing, "gx", 1)
    spread = jax.ops.segment_sum(
        spread_terms(particle_impulse, own_weight), owner_brick, num_segments=total_bricks
    )
    spread = spread + jax.ops.segment_sum(
        spread_terms(particle_impulse, inner_weight), inner_index, num_segments=total_bricks
    )
    spread = spread + received
    spread_field = from_bricks(
        spread.reshape(total_bricks, 3, 64).transpose(1, 0, 2), size_x, size_y, size_z
    )
    velocity_forced = velocity_star + volume_ratio * spread_field
    velocity_new, pressure_potential = project(velocity_forced)
    return (velocity_new, pressure_potential, particle_impulse)


def solution(mesh):
    placed = (
        P(None, "gx", "gy", None),
        P(("gx", "gy")),
        P(("gx", "gy")),
        P(("gx", "gy"), None),
        P(None, ("gx", "gy")),
        P(None, ("gx", "gy")),
    )
    return jax.shard_map(
        body,
        mesh=mesh,
        in_specs=placed,
        out_specs=(P(None, "gx", "gy", None), P("gx", "gy", None), P(None, ("gx", "gy"))),
        check_vma=False,
    )
```

profile of v0, /device:TPU:1, one launch (start us, length us, event | category | flops | bytes accessed | tf_op | source)
XLA Modules:
  0.0 121.3 jit_solution(141779033522570166)
XLA Ops:
  0.6 0.8 fusion.12
  1.5 4.5 %collective-permute-start.1 = (f32[3,1,16,256]{3,2,1,0:T(8,128)S(1)}, f32[3,1,16,256]{3,2,1,0:T(8,128)S(1)}, u32[]{:S(2)}, u32[]{:S(2)}) collective-permute-start(f32[3,1,16,256]{3,2,1,0:T(8,128)S(1)} %get-tuple-element.23), channel_id=1, source_target_pairs={{0,8},{8,16},{16,24},{24,32},{32,40},{40,48},{48,56},{56,64},{64,7... | collective-permute-start | bytes 147464 | tf_op jit(solution)/shard_map/ppermute | solution.py:22
  6.0 6.2 %collective-permute-start = (f32[3,1,16,256]{3,2,1,0:T(8,128)S(1)}, f32[3,1,16,256]{3,2,1,0:T(8,128)S(1)}, u32[]{:S(2)}, u32[]{:S(2)}) collective-permute-start(f32[3,1,16,256]{3,2,1,0:T(8,128)S(1)} %get-tuple-element.22), channel_id=1, source_target_pairs={{8,0},{16,8},{24,16},{32,24},{40,32},{48,40},{56,48},{64,56},{72,6... | collective-permute-start | bytes 147464 | tf_op jit(solution)/shard_map/ppermute | solution.py:24
  12.2 0.9 slice_bitcast_fusion.2
  13.1 1.1 fusion.13
  14.2 1.0 fusion.14
  15.3 0.7 compare_select_fusion.1
  16.0 0.7 compare_convert_fusion.1
  16.6 1.0 fusion.6
  17.7 0.9 constant_dynamic-update-slice_fusion.1
  18.7 1.9 %collective-permute-start.2 = (f32[3,6,1,256]{3,2,1,0:T(1,128)S(1)}, f32[3,6,1,256]{3,2,1,0:T(1,128)S(1)}, u32[]{:S(2)}, u32[]{:S(2)}) collective-permute-start(f32[3,6,1,256]{3,2,1,0:T(1,128)S(1)} %get-tuple-element.17), channel_id=1, source_target_pairs={{1,0},{2,1},{3,2},{4,3},{5,4},{6,5},{7,6},{0,7},{9,8},{10,9},{11,1... | collective-permute-start | bytes 55304 | tf_op jit(solution)/shard_map/ppermute | solution.py:24
  20.6 3.4 %collective-permute-start.3 = (f32[3,6,1,256]{3,2,1,0:T(1,128)S(1)}, f32[3,6,1,256]{3,2,1,0:T(1,128)S(1)}, u32[]{:S(2)}, u32[]{:S(2)}) collective-permute-start(f32[3,6,1,256]{3,2,1,0:T(1,128)S(1)} %get-tuple-element.18), channel_id=1, source_target_pairs={{0,1},{1,2},{2,3},{3,4},{4,5},{5,6},{6,7},{7,0},{8,9},{9,10},{10,1... | collective-permute-start | bytes 55304 | tf_op jit(solution)/shard_map/ppermute | solution.py:22
  24.0 2.3 %collective-permute-done.3 = f32[3,6,1,256]{3,2,1,0:T(1,128)S(1)} collective-permute-done((f32[3,6,1,256]{3,2,1,0:T(1,128)S(1)}, f32[3,6,1,256]{3,2,1,0:T(1,128)S(1)}, u32[]{:S(2)}, u32[]{:S(2)}) %collective-permute-start.3) | collective-permute-done | bytes 18464 | tf_op jit(solution)/shard_map/ppermute | solution.py:22
  26.4 1.3 %multiply_add_fusion = f32[3,4,16,256]{3,2,1,0:T(8,128)S(1)} fusion(f32[3,4,16,256]{3,2,1,0:T(8,128)} %param.14, f32[3,4,16,255]{3,2,1,0:T(8,128)S(1)} %get-tuple-element.25, f32[3,4,16,1]{3,2,1,0:T(8,128)S(1)} %get-tuple-element.27, f32[3,4,16,1]{3,2,1,0:T(8,128)S(1)} %get-tuple-element.26, f32[3,4,16,255]{3,2,1,0:T(8,128)S(1)} %get-tuple-element.24, ...), kind=kLoop, calls=%fused_computation.16 | loop fusion | flops 1277952 | bytes 1413120 | tf_op jit(solution)/shard_map/add | solution.py:396
  27.7 7.8 %reshape.44 = f32[3,1,4,4,4,64,4]{6,5,4,3,2,0,1:T(8,128)} reshape(f32[3,4,16,256]{3,2,1,0:T(8,128)S(1)} %multiply_add_fusion) | data formatting | bytes 393216 | tf_op jit(solution)/shard_map/reshape | solution.py:38
  35.5 4.6 %copy.56 = f32[3,1,4,64,4,4,4]{3,2,6,5,4,0,1:T(4,128)S(1)} copy(f32[3,1,4,64,4,4,4]{6,3,5,2,4,0,1:T(8,128)} %bitcast.31) | data formatting | bytes 393216 | tf_op jit(solution)/shard_map/transpose | solution.py:39
  40.1 0.3 reshape.45
  40.4 0.2 copy.57
  40.6 11.8 %collective-permute-start.4 = (f32[3,256,64]{2,0,1:T(4,128)S(1)}, f32[3,256,64]{2,0,1:T(4,128)S(1)}, u32[]{:S(2)}, u32[]{:S(2)}) collective-permute-start(f32[3,256,64]{2,0,1:T(4,128)S(1)} %copy.57), channel_id=1, source_target_pairs={{0,504},{8,0},{16,8},{24,16},{32,24},{40,32},{48,40},{56,48},{64,5... | collective-permute-start | bytes 589832 | tf_op jit(solution)/shard_map/ppermute | solution.py:33
  52.5 0.8 gather_fusion
  53.2 0.2 multiply_reduce_fusion.2
  53.4 0.1 copy.59
  53.5 0.8 gather_fusion.1
  54.3 0.2 multiply_reduce_fusion.1
  54.5 0.1 copy.60
  54.5 0.8 gather_fusion.2
  55.3 0.2 multiply_reduce_fusion
  55.6 0.1 copy.63
  55.8 0.2 broadcast_multiply_fusion.1
  56.0 0.1 copy.68
  56.1 0.1 copy.69
  56.2 1.3 %scatter_custom_fusion.2 = f32[256,192]{1,0:T(8,128)S(1)} fusion(s32[128]{0:T(128)S(1)} %get-tuple-element.37, f32[128,192]{1,0:T(8,128)S(1)} %copy.69, f32[]{:T(128)} %constant.53.clone.1), kind=kCustom, calls=%fused_computation.20 | custom fusion | flops 24576 | bytes 196612 | tf_op jit(solution)/shard_map/scatter-add | solution.py:425
  57.5 1.9 %collective-permute-start.5 = (f32[256,192]{1,0:T(8,128)S(1)}, f32[256,192]{1,0:T(8,128)S(1)}, u32[]{:S(2)}, u32[]{:S(2)}) collective-permute-start(f32[256,192]{1,0:T(8,128)S(1)} %scatter_custom_fusion.2), channel_id=1, source_target_pairs={{0,8},{8,16},{16,24},{24,32},{32,40},{40,48},{48,56},{56,64},{64,7... | collective-permute-start | bytes 589832 | tf_op jit(solution)/shard_map/ppermute | solution.py:33
  59.5 0.1 copy.66
  59.6 0.1 copy.67
  59.7 0.1 copy.64
  59.8 0.1 copy.65
  59.9 1.4 %scatter_custom_fusion = f32[256,192]{1,0:T(8,128)S(1)} fusion(s32[128]{0:T(128)} %param.15, f32[128,192]{1,0:T(8,128)S(1)} %copy.65, f32[]{:T(128)} %constant.53.clone.1), kind=kCustom, calls=%fused_computation.24 | custom fusion | flops 24576 | bytes 197120 | tf_op jit(solution)/shard_map/scatter-add | solution.py:429
  61.4 1.3 %scatter_custom_fusion.1 = f32[256,192]{1,0:T(8,128)S(1)} fusion(s32[128]{0:T(128)S(1)} %get-tuple-element.11, f32[128,192]{1,0:T(8,128)S(1)} %copy.67, f32[]{:T(128)} %constant.53.clone.1), kind=kCustom, calls=%fused_computation.22 | custom fusion | flops 24576 | bytes 196612 | tf_op jit(solution)/shard_map/scatter-add | solution.py:432
  62.7 2.3 %collective-permute-done.5 = f32[256,192]{1,0:T(8,128)S(1)} collective-permute-done((f32[256,192]{1,0:T(8,128)S(1)}, f32[256,192]{1,0:T(8,128)S(1)}, u32[]{:S(2)}, u32[]{:S(2)}) %collective-permute-start.5) | collective-permute-done | bytes 196640 | tf_op jit(solution)/shard_map/ppermute | solution.py:33
  65.1 0.1 copy.70
  65.2 0.2 mul.225
  65.4 4.1 %copy.71 = f32[3,1,4,4,4,64,4]{6,5,4,3,2,0,1:T(8,128)} copy(f32[3,1,4,4,4,64,4]{5,3,6,4,2,0,1:T(4,128)S(1)} %bitcast.32) | data formatting | bytes 393216 | tf_op jit(solution)/shard_map/mul | solution.py:439
  69.5 6.6 %mul.227 = f32[3,4,16,256]{3,2,1,0:T(8,128)S(1)} reshape(f32[3,1,4,4,4,64,4]{6,5,4,3,2,0,1:T(8,128)} %copy.71) | data formatting | bytes 393216 | tf_op jit(solution)/shard_map/mul | solution.py:439
  76.1 0.7 add.88.forced
  76.8 41.3 %shard_map.157 = (f32[3,4,16,256]{3,2,1,0:T(8,128)}, f32[4,16,256]{2,1,0:T(8,128)}) custom-call(f32[3,4,16,256]{3,2,1,0:T(8,128)} %add.88.forced, bf16[2,256,256]{2,1,0:T(8,128)(2,1)} %constant.62.clone.depth_hbm, bf16[2,256,256]{2,1,0:T(8,128)(2,1)} %constant.63.clone.depth_back_hbm, bf16[2,2,192,256]{3,2,1,0:T(8,128)(2,1)} %constant.64.clone.rows_hbm, ...), custom_call_target="tpu_custom_call" | custom-call | tf_op jit(solution)/shard_map/pallas_call | solution.py:351
  118.2 1.6 %copy.76 = f32[3,4,16,256]{3,2,1,0:T(8,128)} copy(f32[3,4,16,256]{3,2,1,0:T(8,128)} %get-tuple-element.43) | data formatting | bytes 393216
  119.8 1.5 %copy.77 = f32[4,16,256]{2,1,0:T(8,128)} copy(f32[4,16,256]{2,1,0:T(8,128)} %get-tuple-element.44) | data formatting | bytes 131072
  (19 shorter events, 0.2 us)
Async XLA Ops:
  1.5 16.2 %collective-permute-start.1 = (f32[3,1,16,256]{3,2,1,0:T(8,128)S(1)}, f32[3,1,16,256]{3,2,1,0:T(8,128)S(1)}, u32[]{:S(2)}, u32[]{:S(2)}) collective-permute-start(f32[3,1,16,256]{3,2,1,0:T(8,128)S(1)} %get-tuple-element.23), channel_id=1, source_target_pairs={{0,8},{8,16},{16,24},{24,32},{32,40},{40,48},{48,56},{56,64},{64,7... | collective-permute-start | bytes 147464 | tf_op jit(solution)/shard_map/ppermute | solution.py:22
  6.0 12.7 %collective-permute-start = (f32[3,1,16,256]{3,2,1,0:T(8,128)S(1)}, f32[3,1,16,256]{3,2,1,0:T(8,128)S(1)}, u32[]{:S(2)}, u32[]{:S(2)}) collective-permute-start(f32[3,1,16,256]{3,2,1,0:T(8,128)S(1)} %get-tuple-element.22), channel_id=1, source_target_pairs={{8,0},{16,8},{24,16},{32,24},{40,32},{48,40},{56,48},{64,56},{72,6... | collective-permute-start | bytes 147464 | tf_op jit(solution)/shard_map/ppermute | solution.py:24
  18.7 5.3 %collective-permute-start.2 = (f32[3,6,1,256]{3,2,1,0:T(1,128)S(1)}, f32[3,6,1,256]{3,2,1,0:T(1,128)S(1)}, u32[]{:S(2)}, u32[]{:S(2)}) collective-permute-start(f32[3,6,1,256]{3,2,1,0:T(1,128)S(1)} %get-tuple-element.17), channel_id=1, source_target_pairs={{1,0},{2,1},{3,2},{4,3},{5,4},{6,5},{7,6},{0,7},{9,8},{10,9},{11,1... | collective-permute-start | bytes 55304 | tf_op jit(solution)/shard_map/ppermute | solution.py:24
  20.6 5.7 %collective-permute-start.3 = (f32[3,6,1,256]{3,2,1,0:T(1,128)S(1)}, f32[3,6,1,256]{3,2,1,0:T(1,128)S(1)}, u32[]{:S(2)}, u32[]{:S(2)}) collective-permute-start(f32[3,6,1,256]{3,2,1,0:T(1,128)S(1)} %get-tuple-element.18), channel_id=1, source_target_pairs={{0,1},{1,2},{2,3},{3,4},{4,5},{5,6},{6,7},{7,0},{8,9},{9,10},{10,1... | collective-permute-start | bytes 55304 | tf_op jit(solution)/shard_map/ppermute | solution.py:22
  35.5 20.1 %copy-start.1 = (f32[3,128]{1,0:T(4,128)S(1)}, f32[3,128]{1,0:T(4,128)}, u32[]{:S(2)}) copy-start(f32[3,128]{1,0:T(4,128)} %param.18) | copy-start | bytes 4612
  35.5 20.1 %copy-start.2 = (f32[3,128]{1,0:T(4,128)S(1)}, f32[3,128]{1,0:T(4,128)}, u32[]{:S(2)}) copy-start(f32[3,128]{1,0:T(4,128)} %param.19) | copy-start | bytes 4612
  40.6 13.9 %collective-permute-start.4 = (f32[3,256,64]{2,0,1:T(4,128)S(1)}, f32[3,256,64]{2,0,1:T(4,128)S(1)}, u32[]{:S(2)}, u32[]{:S(2)}) collective-permute-start(f32[3,256,64]{2,0,1:T(4,128)S(1)} %copy.57), channel_id=1, source_target_pairs={{0,504},{8,0},{16,8},{24,16},{32,24},{40,32},{48,40},{56,48},{64,5... | collective-permute-start | bytes 589832 | tf_op jit(solution)/shard_map/ppermute | solution.py:33
  55.6 20.5 %copy-start = (f32[3,128]{1,0:T(4,128)}, f32[3,128]{1,0:T(4,128)S(1)}, u32[]{:S(2)}) copy-start(f32[3,128]{1,0:T(4,128)S(1)} %fusion.9) | copy-start | bytes 4612
  57.5 7.5 %collective-permute-start.5 = (f32[256,192]{1,0:T(8,128)S(1)}, f32[256,192]{1,0:T(8,128)S(1)}, u32[]{:S(2)}, u32[]{:S(2)}) collective-permute-start(f32[256,192]{1,0:T(8,128)S(1)} %scatter_custom_fusion.2), channel_id=1, source_target_pairs={{0,8},{8,16},{16,24},{24,32},{32,40},{40,48},{48,56},{56,64},{64,7... | collective-permute-start | bytes 589832 | tf_op jit(solution)/shard_map/ppermute | solution.py:33
where the time goes:
time: 122 us; the launch traced here: 121 us
  Pallas kernels  41.3 us (34%)
  local copies, waits for them, and re-layouts  35.2 us (29%)
  starting transfers between devices  29.7 us (24%)
  other arithmetic  9.45 us (8%)
  waiting for transfers between devices  4.66 us (4%)
    pallas_call x1, Pallas kernels, project(): pl.pallas_call(project_kernel, out_shape=(jax.ShapeDtypeStruct((3, 4, 16,...  41.3 us
    ppermute x2, starting transfers between devices, shifted(): lax.ppermute(array, axis, [(i, (i + by) % devices) for i in range(devices)])  13.7 us
    mul x4, local copies, waits for them, and re-layouts, body(): velocity_forced = velocity_star + volume_ratio * spread_field  11 us
    ppermute x2, starting transfers between devices, padded_2(): lax.ppermute(head, axis, [((i + 1) % count, i) for i in range(count)])  8.12 us
    ppermute x2, starting transfers between devices, padded_2(): lax.ppermute(tail, axis, [(i, (i + 1) % count) for i in range(count)])  7.86 us
    reshape x1, local copies, waits for them, and re-layouts, to_bricks(): grid_field.reshape(components, size_x // 4, 4, size_y // 4, 4, size_z //...  7.83 us
    transpose x1, local copies, waits for them, and re-layouts, to_bricks(): blocks = blocks.transpose(0, 1, 3, 5, 2, 4, 6)  4.6 us
    unnamed x10, local copies, waits for them, and re-layouts  4.05 us
  transfers between devices with their start and end apart: 6, of which 2 were waited for; matrix products, arithmetic and copies ran while one was open for 10% of the time, Pallas kernels for 0%

commit v1 on v0

--- a/solution.py
+++ b/solution.py
@@ -10,46 +10,6 @@
 time_step = 0.05
 viscosity = 2.0
 volume_ratio = 16.0
-
-
-def padded_2(cells, sides, width):
-    for axis, dim in sides:
-        count = lax.axis_size(axis)
-        head = lax.slice_in_dim(cells, 0, width, axis=dim)
-        tail = lax.slice_in_dim(cells, cells.shape[dim] - width, cells.shape[dim], axis=dim)
-        cells = jnp.concatenate(
-            [
-                lax.ppermute(tail, axis, [(i, (i + 1) % count) for i in range(count)]),
-                cells,
-                lax.ppermute(head, axis, [((i + 1) % count, i) for i in range(count)]),
-            ],
-            axis=dim,
-        )
-    return cells
-
-
-def shifted(array, axis, by):
-    devices = lax.axis_size(axis)
-    return lax.ppermute(array, axis, [(i, (i + by) % devices) for i in range(devices)])
-
-
-def to_bricks(grid_field):
-    components, size_x, size_y, size_z = grid_field.shape
-    blocks = grid_field.reshape(components, size_x // 4, 4, size_y // 4, 4, size_z // 4, 4)
-    blocks = blocks.transpose(0, 1, 3, 5, 2, 4, 6)
-    return blocks.reshape(components, size_x // 4 * (size_y // 4) * (size_z // 4), 64)
-
-
-def from_bricks(blocks, size_x, size_y, size_z):
-    components = blocks.shape[0]
-    grid_field = blocks.reshape(components, size_x // 4, size_y // 4, size_z // 4, 4, 4, 4)
-    grid_field = grid_field.transpose(0, 1, 4, 2, 5, 3, 6)
-    return grid_field.reshape(components, size_x, size_y, size_z)
-
-
-def spread_terms(impulse, weight):
-    return (impulse.T[:, :, None] * weight[:, None, :]).reshape(weight.shape[0], 192)
-
 
 MESH = pl.DeviceIdType.MESH
 GX, GY = 64, 8
@@ -86,6 +46,9 @@
             columns[px, :, :, xi] = cas_128[:, (2 * np.arange(64) + xi - px) % 128]
     columns = columns.reshape(2, 128, 192)
 
+    n, kk, i, y = np.indices((2, 4, 4, 16)).reshape(4, 512)
+    cells = np.arange(128) == (64 * n + 16 * i + 4 * (y % 4) + kk)[:, None]
+
     def both(tables):
         return np.stack([in_two(table) for table in tables])
 
@@ -94,6 +57,7 @@
     symbol_xz = (square_128[:, None] + square_128[None, :]).astype(np.float32)
     symbol_y = np.broadcast_to(square_64[:, None], (64, 128)).astype(np.float32)
     return (
+        cells.astype(ml_dtypes.bfloat16),
         in_two(depth),
         in_two(depth.T),
         both(rows),
@@ -171,6 +135,39 @@
     pltpu.make_async_copy(source.at[moved], target.at[moved], send_sem).wait()
 
 
+def dot_across(left, right):
+    return lax.dot_general(
+        left, right, (((1,), (1,)), ((), ())), preferred_element_type=jnp.float32
+    )
+
+
+def spread_weights(cells, weights, bricks, shown):
+    top, rest = halves(weights)
+    found = dot_across(cells, top) + dot_across(cells, rest)
+    row = lax.broadcasted_iota(jnp.int32, (64, 128), 0)
+    mask = (lax.rem(row, 16) // 4 == bricks // 64) & shown
+    return [jnp.where(mask, found[64 * k : 64 * k + 64], 0.0) for k in range(4)]
+
+
+def depth_cells(bricks):
+    first = 4 * lax.rem(bricks, 64)
+    wanted = jnp.concatenate([first + k for k in range(4)], axis=1)
+    z = lax.broadcasted_iota(jnp.int32, (256, 512), 0)
+    return jnp.where(z == wanted, 1.0, 0.0).astype(jnp.bfloat16)
+
+
+def spread(impulse, weights, selector):
+    terms = jnp.concatenate(
+        [
+            jnp.concatenate([weights[k] * impulse[c : c + 1] for k in range(4)], axis=1)
+            for c in range(3)
+        ],
+        axis=0,
+    )
+    top, rest = halves(terms)
+    return dot_across(top, selector) + dot_across(rest, selector)
+
+
 def place_of(px, xi):
     return 2 * xi + 1 - px
 
@@ -186,8 +183,14 @@
     )
 
 
-def project_kernel(
-    forced,
+def step_kernel(
+    velocity,
+    bricks,
+    flags,
+    weights_hbm,
+    target_velocity,
+    contact_force,
+    cells,
     depth_hbm,
     depth_back_hbm,
     rows_hbm,
@@ -198,12 +201,22 @@
     symbol_y,
     velocity_new,
     potential,
+    impulse_out,
     depth,
     depth_back,
     rows,
     rows_back,
     columns,
     columns_back,
+    region,
+    weights,
+    weights_below,
+    bricks_below,
+    flags_below,
+    star,
+    impulse,
+    impulse_below,
+    forced,
     padded,
     classes,
     line_out,
@@ -215,6 +228,8 @@
     line_back,
     line_home,
     table_sem,
+    near_send,
+    near_recv,
     own_sem,
     send_sem,
     recv_sem,
@@ -233,13 +248,18 @@
                 (rows_back_hbm.at[py], rows_back),
                 (columns_hbm.at[px], columns),
                 (columns_back_hbm.at[px], columns_back),
+                (velocity, region.at[:, pl.ds(1, 4), pl.ds(8, 16)]),
+                (weights_hbm, weights),
             )
         )
     ]
-    for load in loads:
-        load.start()
+    for number in (6, 7, 0, 2, 4, 5, 3, 1):
+        loads[number].start()
     line_in[...] = jnp.zeros_like(line_in)
     barrier = pltpu.get_barrier_semaphore()
+
+    def away(dx, dy):
+        return (lax.rem(s + GX + dx, GX), lax.rem(t + GY + dy, GY))
 
     def greet_gx(step, carry):
         pl.semaphore_signal(
@@ -253,8 +273,93 @@
         )
         return carry
 
+    for dy in (-1, 1):
+        pl.semaphore_signal(barrier, inc=1, device_id=away(1, dy), device_id_type=MESH)
     lax.fori_loop(1, GY, greet_gy, 0)
     lax.fori_loop(1, GX, greet_gx, 0)
+    pl.semaphore_wait(barrier, GX - 1 + GY - 1 + 2)
+
+    near = [
+        pltpu.make_async_remote_copy(
+            src_ref=source,
+            dst_ref=target,
+            send_sem=near_send.at[number],
+            recv_sem=near_recv.at[number],
+            device_id=away(*where),
+            device_id_type=MESH,
+        )
+        for number, (source, target, where) in enumerate(
+            (
+                (velocity, region.at[:, pl.ds(5, 4), pl.ds(8, 16)], (-1, 0)),
+                (velocity.at[:, pl.ds(3, 1)], region.at[:, pl.ds(0, 1), pl.ds(8, 16)], (1, 0)),
+                (velocity.at[:, pl.ds(0, 1)], region.at[:, pl.ds(9, 1), pl.ds(8, 16)], (-2, 0)),
+                (velocity.at[:, :, pl.ds(0, 1)], region.at[:, pl.ds(1, 4), pl.ds(24, 1)], (0, -1)),
+                (velocity.at[:, :, pl.ds(0, 1)], region.at[:, pl.ds(5, 4), pl.ds(24, 1)], (-1, -1)),
+                (velocity.at[:, :, pl.ds(15, 1)], region.at[:, pl.ds(1, 4), pl.ds(7, 1)], (0, 1)),
+                (velocity.at[:, :, pl.ds(15, 1)], region.at[:, pl.ds(5, 4), pl.ds(7, 1)], (-1, 1)),
+                (weights_hbm, weights_below, (1, 0)),
+                (bricks, bricks_below, (1, 0)),
+                (flags, flags_below, (1, 0)),
+                (impulse, impulse_below, (1, 0)),
+            )
+        )
+    ]
+    for number in range(10):
+        near[number].start()
+
+    loads[7].wait()
+    own_bricks = bricks[...]
+    live = flags[...] > 0
+    own_weights = spread_weights(cells[0:256], weights[...], own_bricks, live)
+    next_weights = spread_weights(cells[256:512], weights[...], own_bricks, flags[...] == 2)
+    selector = depth_cells(own_bricks)
+    for number in (6,):
+        loads[number].wait()
+    for number in range(7):
+        near[number].wait_recv()
+    for x in range(1, 9):
+        block, inner = (x - 1) // 4, (x - 1) % 4
+        centers = [region[c, x, 8:24] for c in range(3)]
+        for c in range(3):
+            v = centers[c]
+            uppers = (region[c, x + 1, 8:24], region[c, x, 9:25], pltpu.roll(v, 255, 1))
+            lowers = (region[c, x - 1, 8:24], region[c, x, 7:23], pltpu.roll(v, 1, 1))
+            laplace = -6.0 * v
+            carried = jnp.zeros_like(v)
+            for d in range(3):
+                laplace = laplace + (uppers[d] + lowers[d])
+                carried = carried + centers[d] * (uppers[d] - lowers[d])
+            base = 192 * block + 64 * c + 16 * inner
+            star[base : base + 16] = v + time_step * (viscosity * laplace - 0.5 * carried)
+
+    top, rest = halves(star[...])
+    found = dot(top, selector) + dot(rest, selector)
+    for c in range(3):
+        total = jnp.zeros((64, 128), jnp.float32)
+        for block, part in enumerate((own_weights, next_weights)):
+            base = 192 * block + 64 * c
+            for k in range(4):
+                total = total + found[base : base + 64, 128 * k : 128 * k + 128] * part[k]
+        interpolated = jnp.sum(total, axis=0, keepdims=True)
+        wanted = target_velocity[c : c + 1] + time_step * contact_force[c : c + 1]
+        impulse[c : c + 1] = jnp.where(live, wanted - interpolated, 0.0)
+    near[10].start()
+    impulse_out[...] = impulse[...]
+    at_home = spread(impulse[...], own_weights, selector)
+    for number in (7, 8, 9):
+        near[number].wait_recv()
+    weights_from = spread_weights(
+        cells[256:512], weights_below[...], bricks_below[...], flags_below[...] == 2
+    )
+    selector_from = depth_cells(bricks_below[...])
+    near[10].wait_recv()
+    from_below = spread(impulse_below[...], weights_from, selector_from)
+    for c in range(3):
+        for x in range(4):
+            base = 64 * c + 16 * x
+            forced[c, x] = star[base : base + 16] + volume_ratio * (
+                at_home[base : base + 16] + from_below[base : base + 16]
+            )
 
     classes[...] = jnp.zeros_like(classes)
     row_number = lax.broadcasted_iota(jnp.int32, (16, 256), 0)
@@ -292,7 +397,6 @@
         line_out[32 * c : 32 * c + 32] = spectrum[
             32 * (c // 2) : 32 * (c // 2) + 32, 128 * (c % 2) : 128 * (c % 2) + 128
         ]
-    pl.semaphore_wait(barrier, GX - 1 + GY - 1)
     exchange_gy(s, t, line_out, line_in, own_sem.at[0], send_sem.at[0], recv_sem.at[0])
 
     loads[2].wait()
@@ -341,21 +445,26 @@
             take(padded, base + 9, 16) - take(padded, base + 7, 16)
         )
         velocity_new[2, x] = forced[2, x] - 0.5 * (pltpu.roll(p, 255, 1) - pltpu.roll(p, 1, 1))
-
-
-def project(forced):
+    for copy in near:
+        copy.wait_send()
+
+
+def step(velocity, owner_brick, particle_flags, weights, target_velocity, contact_force):
     tables = build_tables()
     inside = pl.BlockSpec(memory_space=pltpu.VMEM)
     anywhere = pl.BlockSpec(memory_space=pl.ANY)
     f32, bf16 = jnp.float32, jnp.bfloat16
     return pl.pallas_call(
-        project_kernel,
+        step_kernel,
         out_shape=(
             jax.ShapeDtypeStruct((3, 4, 16, 256), f32),
             jax.ShapeDtypeStruct((4, 16, 256), f32),
+            jax.ShapeDtypeStruct((3, 128), f32),
         ),
-        in_specs=[inside] + [anywhere] * 6 + [inside] * 2,
-        out_specs=(inside, inside),
+        in_specs=[anywhere, inside, inside, anywhere, inside, inside, inside]
+        + [anywhere] * 6
+        + [inside] * 2,
+        out_specs=(inside, inside, inside),
         scratch_shapes=[
             pltpu.VMEM((2, 256, 256), bf16),
             pltpu.VMEM((2, 256, 256), bf16),
@@ -363,6 +472,15 @@
             pltpu.VMEM((2, 256, 192), bf16),
             pltpu.VMEM((2, 128, 192), bf16),
             pltpu.VMEM((2, 192, 128), bf16),
+            pltpu.VMEM((3, 10, 32, 256), f32),
+            pltpu.VMEM((128, 128), f32),
+            pltpu.VMEM((128, 128), f32),
+            pltpu.VMEM((1, 128), jnp.int32),
+            pltpu.VMEM((1, 128), jnp.int32),
+            pltpu.VMEM((384, 256), f32),
+            pltpu.VMEM((3, 128), f32),
+            pltpu.VMEM((3, 128), f32),
+            pltpu.VMEM((3, 4, 16, 256), f32),
             pltpu.VMEM((2, 192, 128), f32),
             pltpu.VMEM((128, 256), f32),
             pltpu.VMEM((256, 128), f32),
@@ -373,72 +491,25 @@
             pltpu.VMEM((192, 128), f32),
             pltpu.VMEM((256, 128), f32),
             pltpu.VMEM((256, 128), f32),
-            pltpu.SemaphoreType.DMA((6,)),
+            pltpu.SemaphoreType.DMA((8,)),
+            pltpu.SemaphoreType.DMA((11,)),
+            pltpu.SemaphoreType.DMA((11,)),
             pltpu.SemaphoreType.DMA((4,)),
             pltpu.SemaphoreType.DMA((4,)),
             pltpu.SemaphoreType.DMA((4,)),
         ],
-        compiler_params=pltpu.CompilerParams(collective_id=0, has_side_effects=True),
-    )(forced, *[jnp.asarray(table) for table in tables])
-
-
-def advance(velocity):
-    padded = padded_2(velocity, (("gx", 1), ("gy", 2)), 1)
-    uppers = (padded[:, 2:, 1:-1], padded[:, 1:-1, 2:], jnp.roll(velocity, -1, 3))
-    lowers = (padded[:, :-2, 1:-1], padded[:, 1:-1, :-2], jnp.roll(velocity, 1, 3))
-    laplace = -6.0 * velocity
-    carried = jnp.zeros_like(velocity)
-    for direction in range(3):
-        laplace = laplace + uppers[direction] + lowers[direction]
-        carried = (
-            carried + velocity[direction][None] * (uppers[direction] - lowers[direction]) * 0.5
-        )
-    return velocity + time_step * (viscosity * laplace - carried)
-
-
-def body(velocity, owner_brick, particle_flags, weights, target_velocity, contact_force):
-    size_x = velocity.shape[1]
-    size_y = velocity.shape[2]
-    size_z = velocity.shape[3]
-    velocity_star = advance(velocity)
-    bricks_x = size_x // 4
-    layer_size = size_y // 4 * (size_z // 4)
-    total_bricks = bricks_x * layer_size
-    star_bricks = to_bricks(velocity_star)
-    block_x = owner_brick // layer_size
-    in_layer = owner_brick % layer_size
-    inside = block_x < bricks_x - 1
-    live_mask = (particle_flags > 0).astype(jnp.float32)
-    crossing = (particle_flags == 2).astype(jnp.float32)
-    own_weight = weights[:, :64] * live_mask[:, None]
-    next_weight = weights[:, 64:] * crossing[:, None]
-    inner_weight = next_weight * inside.astype(jnp.float32)[:, None]
-    outer_weight = next_weight - inner_weight
-    inner_index = jnp.where(inside, owner_brick + layer_size, owner_brick)
-    interpolated = jnp.sum(star_bricks[:, owner_brick] * own_weight[None], axis=2)
-    interpolated = interpolated + jnp.sum(star_bricks[:, inner_index] * inner_weight[None], axis=2)
-    from_next = shifted(star_bricks, "gx", -1)
-    interpolated = interpolated + jnp.sum(from_next[:, in_layer] * outer_weight[None], axis=2)
-    particle_impulse = live_mask[None] * (
-        target_velocity - interpolated + time_step * contact_force
-    )
-    outgoing = jax.ops.segment_sum(
-        spread_terms(particle_impulse, outer_weight), in_layer, num_segments=layer_size
-    )
-    received = shifted(outgoing, "gx", 1)
-    spread = jax.ops.segment_sum(
-        spread_terms(particle_impulse, own_weight), owner_brick, num_segments=total_bricks
-    )
-    spread = spread + jax.ops.segment_sum(
-        spread_terms(particle_impulse, inner_weight), inner_index, num_segments=total_bricks
-    )
-    spread = spread + received
-    spread_field = from_bricks(
-        spread.reshape(total_bricks, 3, 64).transpose(1, 0, 2), size_x, size_y, size_z
-    )
-    velocity_forced = velocity_star + volume_ratio * spread_field
-    velocity_new, pressure_potential = project(velocity_forced)
-    return (velocity_new, pressure_potential, particle_impulse)
+        compiler_params=pltpu.CompilerParams(
+            collective_id=0, has_side_effects=True, vmem_limit_bytes=32 * 1024 * 1024
+        ),
+    )(
+        velocity,
+        owner_brick.reshape(1, 128),
+        particle_flags.reshape(1, 128),
+        weights,
+        target_velocity,
+        contact_force,
+        *[jnp.asarray(table) for table in tables],
+    )
 
 
 def solution(mesh):
@@ -451,7 +522,7 @@
         P(None, ("gx", "gy")),
     )
     return jax.shard_map(
-        body,
+        step,
         mesh=mesh,
         in_specs=placed,
         out_specs=(P(None, "gx", "gy", None), P("gx", "gy", None), P(None, ("gx", "gy"))),

time: 122 us -> 67.1 us (0.55)
  starting transfers between devices: 29.7 us -> 0 us
  local copies, waits for them, and re-layouts: 35.2 us -> 13.3 us
  Pallas kernels: 41.3 us -> 52.5 us
  other arithmetic: 9.45 us -> 0 us
  waiting for transfers between devices: 4.66 us -> 0 us
    ppermute x6 -> x0, starting transfers between devices: 29.7 us -> none  [the longest x2 13.7 us: shifted(): lax.ppermute(array, axis, [(i, (i + by) % devices) for i in range(devices)])]
    mul x11 -> x0, local copies, waits for them, and re-layouts: 12.6 us -> none  [the longest x4 11 us: body(): velocity_forced = velocity_star + volume_ratio * spread_field]
    pallas_call x1, Pallas kernels: 41.3 us -> 52.5 us  [step(): pl.pallas_call(step_kernel, out_shape=(jax.ShapeDtypeStruct((3, 4, 16, 25...]
    unnamed x10 -> x33, local copies, waits for them, and re-layouts: 4.05 us -> 13.3 us
    reshape x3 -> x0, local copies, waits for them, and re-layouts: 8.33 us -> none  [the longest x1 7.83 us: to_bricks(): grid_field.reshape(components, size_x // 4, 4, size_y // 4, 4, size_z //...]
    transpose x2 -> x0, local copies, waits for them, and re-layouts: 4.71 us -> none  [the longest x1 4.6 us: to_bricks(): blocks = blocks.transpose(0, 1, 3, 5, 2, 4, 6)]
    ppermute x6 -> x0, waiting for transfers between devices: 4.66 us -> none  [the longest x2 2.33 us: shifted(): lax.ppermute(array, axis, [(i, (i + by) % devices) for i in range(devices)])]
    scatter-add x3 -> x0, other arithmetic: 4.1 us -> none  [the longest x1 1.45 us: body(): jax.ops.segment_sum(spread_terms(particle_impulse, own_weight), owner_bri...]
  transfers between devices with their start and end apart: 6 -> 0, of which waited for: 2 -> 0; matrix products, arithmetic and copies ran while one was open for 10% -> 0% of each run, Pallas kernels for 0% -> 0%
where the time goes in v1:
time: 67.1 us; the launch traced here: 66.5 us
  Pallas kernels  52.5 us (78%)
  local copies, waits for them, and re-layouts  13.3 us (20%)
  between operations  0.68 us (1%)
    pallas_call x1, Pallas kernels, step(): pl.pallas_call(step_kernel, out_shape=(jax.ShapeDtypeStruct((3, 4, 16, 25...  52.5 us
    unnamed x33, local copies, waits for them, and re-layouts  13.3 us

profile of v1, /device:TPU:1, one launch (start us, length us, event | category | flops | bytes accessed | tf_op | source)
XLA Modules:
  0.0 66.5 jit_solution(12003329418634832640)
XLA Ops:
  0.6 0.0 copy-start.11
  0.6 0.0 copy-start.13
  0.7 0.0 copy-start.14
  0.7 0.7 copy-done.11
  1.3 0.0 copy-done.13
  1.3 0.0 copy-done.14
  1.3 0.0 copy-start
  1.3 1.0 %copy-done = bf16[2,2,256,192]{3,2,1,0:T(8,128)(2,1)S(1)} copy-done((bf16[2,2,256,192]{3,2,1,0:T(8,128)(2,1)S(1)}, bf16[2,2,256,192]{3,2,1,0:T(8,128)(2,1)}, u32[]{:S(2)}) %copy-start) | copy-done | bytes 393240
  2.4 0.0 copy-start.1
  2.4 1.0 %copy-done.1 = bf16[2,2,192,256]{3,2,1,0:T(8,128)(2,1)S(1)} copy-done((bf16[2,2,192,256]{3,2,1,0:T(8,128)(2,1)S(1)}, bf16[2,2,192,256]{3,2,1,0:T(8,128)(2,1)}, u32[]{:S(2)}) %copy-start.1) | copy-done | bytes 393240
  3.4 0.0 copy-start.2
  3.4 0.9 %copy-done.2 = bf16[2,2,128,192]{3,2,1,0:T(8,128)(2,1)S(1)} copy-done((bf16[2,2,128,192]{3,2,1,0:T(8,128)(2,1)S(1)}, bf16[2,2,128,192]{3,2,1,0:T(8,128)(2,1)}, u32[]{:S(2)}) %copy-start.2) | copy-done | bytes 196632
  4.3 0.0 copy-start.3
  4.3 0.9 %copy-done.3 = bf16[2,256,256]{2,1,0:T(8,128)(2,1)S(1)} copy-done((bf16[2,256,256]{2,1,0:T(8,128)(2,1)S(1)}, bf16[2,256,256]{2,1,0:T(8,128)(2,1)}, u32[]{:S(2)}) %copy-start.3) | copy-done | bytes 262168
  5.3 0.0 copy-start.4
  5.3 0.9 %copy-done.4 = bf16[2,256,256]{2,1,0:T(8,128)(2,1)S(1)} copy-done((bf16[2,256,256]{2,1,0:T(8,128)(2,1)S(1)}, bf16[2,256,256]{2,1,0:T(8,128)(2,1)}, u32[]{:S(2)}) %copy-start.4) | copy-done | bytes 262168
  6.2 0.0 copy-start.5
  6.2 0.9 %copy-done.5 = f32[3,4,16,256]{3,2,1,0:T(8,128)S(1)} copy-done((f32[3,4,16,256]{3,2,1,0:T(8,128)S(1)}, f32[3,4,16,256]{3,2,1,0:T(8,128)}, u32[]{:S(2)}) %copy-start.5) | copy-done | bytes 196632
  7.1 0.0 copy-start.6
  7.1 0.9 %copy-done.6 = bf16[2,2,192,128]{3,2,1,0:T(8,128)(2,1)S(1)} copy-done((bf16[2,2,192,128]{3,2,1,0:T(8,128)(2,1)S(1)}, bf16[2,2,192,128]{3,2,1,0:T(8,128)(2,1)}, u32[]{:S(2)}) %copy-start.6) | copy-done | bytes 196632
  8.1 0.0 copy-start.7
  8.1 0.9 %copy-done.7 = bf16[512,128]{1,0:T(8,128)(2,1)S(1)} copy-done((bf16[512,128]{1,0:T(8,128)(2,1)S(1)}, bf16[512,128]{1,0:T(8,128)(2,1)}, u32[]{:S(2)}) %copy-start.7) | copy-done | bytes 131096
  9.0 0.0 copy-start.8
  9.0 0.8 %copy-done.8 = f32[128,128]{1,0:T(8,128)S(1)} copy-done((f32[128,128]{1,0:T(8,128)S(1)}, f32[128,128]{1,0:T(8,128)}, u32[]{:S(2)}) %copy-start.8) | copy-done | bytes 65560
  9.8 0.0 copy-start.9
  9.8 0.8 %copy-done.9 = f32[128,128]{1,0:T(8,128)S(1)} copy-done((f32[128,128]{1,0:T(8,128)S(1)}, f32[128,128]{1,0:T(8,128)}, u32[]{:S(2)}) %copy-start.9) | copy-done | bytes 65560
  10.7 0.0 copy-start.10
  10.7 0.8 %copy-done.10 = f32[64,128]{1,0:T(8,128)S(1)} copy-done((f32[64,128]{1,0:T(8,128)S(1)}, f32[64,128]{1,0:T(8,128)}, u32[]{:S(2)}) %copy-start.10) | copy-done | bytes 32792
  11.4 0.0 copy-start.12
  11.4 0.7 %copy-done.12 = f32[3,128]{1,0:T(4,128)S(1)} copy-done((f32[3,128]{1,0:T(4,128)S(1)}, f32[3,128]{1,0:T(4,128)}, u32[]{:S(2)}) %copy-start.12) | copy-done | bytes 1560
  12.1 52.5 %shard_map.166 = (f32[3,4,16,256]{3,2,1,0:T(8,128)S(1)}, f32[4,16,256]{2,1,0:T(8,128)S(1)}, f32[3,128]{1,0:T(4,128)S(1)}) custom-call(f32[3,4,16,256]{3,2,1,0:T(8,128)S(1)} %copy-done.5, s32[1,128]{1,0:T(1,128)S(1)} %bitcast.2, s32[1,128]{1,0:T(1,128)S(1)} %bitcast.3, f32[128,128]{1,0:T(8,128)S(1)} %copy-done.8, f32[3,128]{1,0:T(4,128)S(1)} %copy-done.11, ...), custom_call_target="tpu_custom_call" | custom-call | tf_op jit(solution)/shard_map/pallas_call | solution.py:457
  64.6 0.7 %copy.21 = f32[3,4,16,256]{3,2,1,0:T(8,128)} copy(f32[3,4,16,256]{3,2,1,0:T(8,128)S(1)} %get-tuple-element.6) | data formatting | bytes 393216
  65.3 0.6 copy.22
  65.9 0.6 copy.23
Async XLA Ops:
  0.6 0.7 %copy-start.11 = (f32[3,128]{1,0:T(4,128)S(1)}, f32[3,128]{1,0:T(4,128)}, u32[]{:S(2)}) copy-start(f32[3,128]{1,0:T(4,128)} %target_velocity.1) | copy-start | bytes 4612
  0.6 0.7 %copy-start.13 = (s32[128]{0:T(128)S(1)}, s32[128]{0:T(128)}, u32[]{:S(2)}) copy-start(s32[128]{0:T(128)} %param.16) | copy-start | bytes 1540
  0.7 0.7 %copy-start.14 = (s32[128]{0:T(128)S(1)}, s32[128]{0:T(128)}, u32[]{:S(2)}) copy-start(s32[128]{0:T(128)} %param.17) | copy-start | bytes 1540
  1.3 1.0 %copy-start = (bf16[2,2,256,192]{3,2,1,0:T(8,128)(2,1)S(1)}, bf16[2,2,256,192]{3,2,1,0:T(8,128)(2,1)}, u32[]{:S(2)}) copy-start(bf16[2,2,256,192]{3,2,1,0:T(8,128)(2,1)} %constant.22.clone.rows_back_hbm) | copy-start | bytes 1179652
  2.4 1.0 %copy-start.1 = (bf16[2,2,192,256]{3,2,1,0:T(8,128)(2,1)S(1)}, bf16[2,2,192,256]{3,2,1,0:T(8,128)(2,1)}, u32[]{:S(2)}) copy-start(bf16[2,2,192,256]{3,2,1,0:T(8,128)(2,1)} %constant.21.clone.rows_hbm) | copy-start | bytes 1179652
  3.4 0.9 %copy-start.2 = (bf16[2,2,128,192]{3,2,1,0:T(8,128)(2,1)S(1)}, bf16[2,2,128,192]{3,2,1,0:T(8,128)(2,1)}, u32[]{:S(2)}) copy-start(bf16[2,2,128,192]{3,2,1,0:T(8,128)(2,1)} %constant.23.clone.columns_hbm) | copy-start | bytes 589828
  4.3 0.9 %copy-start.3 = (bf16[2,256,256]{2,1,0:T(8,128)(2,1)S(1)}, bf16[2,256,256]{2,1,0:T(8,128)(2,1)}, u32[]{:S(2)}) copy-start(bf16[2,256,256]{2,1,0:T(8,128)(2,1)} %constant.20.clone.depth_back_hbm) | copy-start | bytes 786436
  5.3 0.9 %copy-start.4 = (bf16[2,256,256]{2,1,0:T(8,128)(2,1)S(1)}, bf16[2,256,256]{2,1,0:T(8,128)(2,1)}, u32[]{:S(2)}) copy-start(bf16[2,256,256]{2,1,0:T(8,128)(2,1)} %constant.19.clone.depth_hbm) | copy-start | bytes 786436
  6.2 0.9 %copy-start.5 = (f32[3,4,16,256]{3,2,1,0:T(8,128)S(1)}, f32[3,4,16,256]{3,2,1,0:T(8,128)}, u32[]{:S(2)}) copy-start(f32[3,4,16,256]{3,2,1,0:T(8,128)} %velocity.1) | copy-start | bytes 589828
  7.1 0.9 %copy-start.6 = (bf16[2,2,192,128]{3,2,1,0:T(8,128)(2,1)S(1)}, bf16[2,2,192,128]{3,2,1,0:T(8,128)(2,1)}, u32[]{:S(2)}) copy-start(bf16[2,2,192,128]{3,2,1,0:T(8,128)(2,1)} %constant.24.clone.columns_back_hbm) | copy-start | bytes 589828
  8.1 0.9 %copy-start.7 = (bf16[512,128]{1,0:T(8,128)(2,1)S(1)}, bf16[512,128]{1,0:T(8,128)(2,1)}, u32[]{:S(2)}) copy-start(bf16[512,128]{1,0:T(8,128)(2,1)} %constant.18.clone.cells) | copy-start | bytes 393220
  9.0 0.8 %copy-start.8 = (f32[128,128]{1,0:T(8,128)S(1)}, f32[128,128]{1,0:T(8,128)}, u32[]{:S(2)}) copy-start(f32[128,128]{1,0:T(8,128)} %weights_hbm.1) | copy-start | bytes 196612
  9.8 0.8 %copy-start.9 = (f32[128,128]{1,0:T(8,128)S(1)}, f32[128,128]{1,0:T(8,128)}, u32[]{:S(2)}) copy-start(f32[128,128]{1,0:T(8,128)} %constant.25.clone.symbol_xz) | copy-start | bytes 196612
  10.7 0.8 %copy-start.10 = (f32[64,128]{1,0:T(8,128)S(1)}, f32[64,128]{1,0:T(8,128)}, u32[]{:S(2)}) copy-start(f32[64,128]{1,0:T(8,128)} %constant.26.clone.symbol_y) | copy-start | bytes 98308
  11.4 0.7 %copy-start.12 = (f32[3,128]{1,0:T(4,128)S(1)}, f32[3,128]{1,0:T(4,128)}, u32[]{:S(2)}) copy-start(f32[3,128]{1,0:T(4,128)} %contact_force.1) | copy-start | bytes 4612

commit v2 on v1

--- a/solution.py
+++ b/solution.py
@@ -89,12 +89,19 @@
     return dot(top, table[0]) + (dot(rest, table[0]) + dot(top, table[1]))
 
 
+def outward(step, size):
+    odd = lax.rem(step, 2)
+    return size // 2 + (1 - odd) * (step // 2) - odd * ((step + 1) // 2)
+
+
 def exchange_gx(s, t, source, target, own_sem, send_sem, recv_sem):
     own = pltpu.make_async_copy(source.at[pl.ds(3 * s, 3)], target.at[pl.ds(3 * s, 3)], own_sem)
     own.start()
 
     def send(step, carry):
-        peer = lax.rem(s + step, GX)
+        z = lax.rem(s // 8 + outward(step // 8, 8), 8)
+        x = lax.rem(lax.rem(s // 2, 4) + outward(lax.rem(step // 2, 4), 4), 4)
+        peer = 8 * z + 2 * x + lax.rem(s + 1 + step, 2)
         pltpu.make_async_remote_copy(
             src_ref=source.at[pl.ds(3 * peer, 3)],
             dst_ref=target.at[pl.ds(3 * s, 3)],
@@ -105,7 +112,7 @@
         ).start()
         return carry
 
-    lax.fori_loop(1, GX, send, 0)
+    lax.fori_loop(0, GX - 1, send, 0)
     own.wait()
     moved = pl.ds(0, 3 * (GX - 1))
     pltpu.make_async_copy(source.at[moved], target.at[moved], recv_sem).wait()
@@ -117,7 +124,7 @@
     own.start()
 
     def send(step, carry):
-        peer = lax.rem(t + step, GY)
+        peer = lax.rem(t + outward(step, GY), GY)
         pltpu.make_async_remote_copy(
             src_ref=source.at[pl.ds(32 * peer, 27)],
             dst_ref=target.at[pl.ds(32 * t, 27)],
@@ -128,7 +135,7 @@
         ).start()
         return carry
 
-    lax.fori_loop(1, GY, send, 0)
+    lax.fori_loop(0, GY - 1, send, 0)
     own.wait()
     moved = pl.ds(0, 27 * (GY - 1))
     pltpu.make_async_copy(source.at[moved], target.at[moved], recv_sem).wait()
@@ -147,6 +154,26 @@
     row = lax.broadcasted_iota(jnp.int32, (64, 128), 0)
     mask = (lax.rem(row, 16) // 4 == bricks // 64) & shown
     return [jnp.where(mask, found[64 * k : 64 * k + 64], 0.0) for k in range(4)]
+
+
+def both_weights(cells, weights, bricks, flags):
+    parts = ((cells[0:256], flags[...] > 0), (cells[256:512], flags[...] == 2))
+    return [spread_weights(part, weights[...], bricks[...], shown) for part, shown in parts]
+
+
+def impulse_of(star, selector, weights, wanted, flags):
+    top, rest = halves(star)
+    found = dot(top, selector) + dot(rest, selector)
+    interpolated = []
+    for c in range(3):
+        total = jnp.zeros((64, 128), jnp.float32)
+        for block in range(2):
+            base = 192 * block + 64 * c
+            for k in range(4):
+                cell = found[base : base + 64, 128 * k : 128 * k + 128]
+                total = total + cell * weights[block][k]
+        interpolated.append(jnp.sum(total, axis=0, keepdims=True))
+    return jnp.where(flags[...] > 0, wanted - jnp.concatenate(interpolated, axis=0), 0.0)
 
 
 def depth_cells(bricks):
@@ -185,23 +212,30 @@
 
 def step_kernel(
     velocity,
-    bricks,
-    flags,
+    bricks_hbm,
+    flags_hbm,
     weights_hbm,
-    target_velocity,
-    contact_force,
-    cells,
+    target_hbm,
+    contact_hbm,
+    cells_hbm,
     depth_hbm,
     depth_back_hbm,
     rows_hbm,
     rows_back_hbm,
     columns_hbm,
     columns_back_hbm,
-    symbol_xz,
-    symbol_y,
+    symbol_xz_hbm,
+    symbol_y_hbm,
     velocity_new,
     potential,
     impulse_out,
+    bricks,
+    flags,
+    target_velocity,
+    contact_force,
+    cells,
+    symbol_xz,
+    symbol_y,
     depth,
     depth_back,
     rows,
@@ -213,9 +247,9 @@
     weights_below,
     bricks_below,
     flags_below,
+    target_below,
+    contact_below,
     star,
-    impulse,
-    impulse_below,
     forced,
     padded,
     classes,
@@ -248,12 +282,19 @@
                 (rows_back_hbm.at[py], rows_back),
                 (columns_hbm.at[px], columns),
                 (columns_back_hbm.at[px], columns_back),
-                (velocity, region.at[:, pl.ds(1, 4), pl.ds(8, 16)]),
+                (velocity, region.at[:, pl.ds(5, 4), pl.ds(8, 16)]),
                 (weights_hbm, weights),
+                (bricks_hbm, bricks),
+                (flags_hbm, flags),
+                (target_hbm, target_velocity),
+                (contact_hbm, contact_force),
+                (cells_hbm, cells),
+                (symbol_xz_hbm, symbol_xz),
+                (symbol_y_hbm.at[pl.ds(s, 1)], symbol_y),
             )
         )
     ]
-    for number in (6, 7, 0, 2, 4, 5, 3, 1):
+    for number in (8, 9, 12, 7, 6, 10, 11, 0, 2, 4, 5, 13, 14, 3, 1):
         loads[number].start()
     line_in[...] = jnp.zeros_like(line_in)
     barrier = pltpu.get_barrier_semaphore()
@@ -273,11 +314,12 @@
         )
         return carry
 
-    for dy in (-1, 1):
-        pl.semaphore_signal(barrier, inc=1, device_id=away(1, dy), device_id_type=MESH)
+    for dx in (-1, 1):
+        for dy in (-1, 1):
+            pl.semaphore_signal(barrier, inc=1, device_id=away(dx, dy), device_id_type=MESH)
     lax.fori_loop(1, GY, greet_gy, 0)
     lax.fori_loop(1, GX, greet_gx, 0)
-    pl.semaphore_wait(barrier, GX - 1 + GY - 1 + 2)
+    pl.semaphore_wait(barrier, GX - 1 + GY - 1 + 4)
 
     near = [
         pltpu.make_async_remote_copy(
@@ -290,34 +332,40 @@
         )
         for number, (source, target, where) in enumerate(
             (
-                (velocity, region.at[:, pl.ds(5, 4), pl.ds(8, 16)], (-1, 0)),
-                (velocity.at[:, pl.ds(3, 1)], region.at[:, pl.ds(0, 1), pl.ds(8, 16)], (1, 0)),
-                (velocity.at[:, pl.ds(0, 1)], region.at[:, pl.ds(9, 1), pl.ds(8, 16)], (-2, 0)),
-                (velocity.at[:, :, pl.ds(0, 1)], region.at[:, pl.ds(1, 4), pl.ds(24, 1)], (0, -1)),
-                (velocity.at[:, :, pl.ds(0, 1)], region.at[:, pl.ds(5, 4), pl.ds(24, 1)], (-1, -1)),
-                (velocity.at[:, :, pl.ds(15, 1)], region.at[:, pl.ds(1, 4), pl.ds(7, 1)], (0, 1)),
-                (velocity.at[:, :, pl.ds(15, 1)], region.at[:, pl.ds(5, 4), pl.ds(7, 1)], (-1, 1)),
+                (velocity.at[:, :, pl.ds(0, 1)], region.at[:, pl.ds(5, 4), pl.ds(24, 1)], (0, -1)),
+                (velocity.at[:, :, pl.ds(0, 1)], region.at[:, pl.ds(9, 4), pl.ds(24, 1)], (-1, -1)),
+                (velocity.at[:, :, pl.ds(0, 1)], region.at[:, pl.ds(1, 4), pl.ds(24, 1)], (1, -1)),
+                (velocity.at[:, :, pl.ds(15, 1)], region.at[:, pl.ds(5, 4), pl.ds(7, 1)], (0, 1)),
+                (velocity.at[:, :, pl.ds(15, 1)], region.at[:, pl.ds(9, 4), pl.ds(7, 1)], (-1, 1)),
+                (velocity.at[:, :, pl.ds(15, 1)], region.at[:, pl.ds(1, 4), pl.ds(7, 1)], (1, 1)),
+                (velocity.at[:, pl.ds(0, 1)], region.at[:, pl.ds(13, 1), pl.ds(8, 16)], (-2, 0)),
+                (velocity.at[:, pl.ds(3, 1)], region.at[:, pl.ds(0, 1), pl.ds(8, 16)], (2, 0)),
+                (bricks_hbm, bricks_below, (1, 0)),
+                (flags_hbm, flags_below, (1, 0)),
+                (target_hbm, target_below, (1, 0)),
+                (contact_hbm, contact_below, (1, 0)),
                 (weights_hbm, weights_below, (1, 0)),
-                (bricks, bricks_below, (1, 0)),
-                (flags, flags_below, (1, 0)),
-                (impulse, impulse_below, (1, 0)),
+                (velocity, region.at[:, pl.ds(9, 4), pl.ds(8, 16)], (-1, 0)),
+                (velocity, region.at[:, pl.ds(1, 4), pl.ds(8, 16)], (1, 0)),
             )
         )
     ]
-    for number in range(10):
-        near[number].start()
-
-    loads[7].wait()
-    own_bricks = bricks[...]
-    live = flags[...] > 0
-    own_weights = spread_weights(cells[0:256], weights[...], own_bricks, live)
-    next_weights = spread_weights(cells[256:512], weights[...], own_bricks, flags[...] == 2)
-    selector = depth_cells(own_bricks)
-    for number in (6,):
+    for copy in near:
+        copy.start()
+
+    for number in (8, 9, 12, 7):
         loads[number].wait()
-    for number in range(7):
+    own_weights, next_weights = both_weights(cells, weights, bricks, flags)
+    selector = depth_cells(bricks[...])
+    for number in (8, 9, 12):
         near[number].wait_recv()
-    for x in range(1, 9):
+    below_weights, here_weights = both_weights(cells, weights_below, bricks_below, flags_below)
+    selector_below = depth_cells(bricks_below[...])
+    for number in (6, 10, 11):
+        loads[number].wait()
+    for number in (0, 1, 2, 3, 4, 5, 6, 7, 10, 11, 13, 14):
+        near[number].wait_recv()
+    for x in range(1, 13):
         block, inner = (x - 1) // 4, (x - 1) % 4
         centers = [region[c, x, 8:24] for c in range(3)]
         for c in range(3):
@@ -332,32 +380,27 @@
             base = 192 * block + 64 * c + 16 * inner
             star[base : base + 16] = v + time_step * (viscosity * laplace - 0.5 * carried)
 
-    top, rest = halves(star[...])
-    found = dot(top, selector) + dot(rest, selector)
-    for c in range(3):
-        total = jnp.zeros((64, 128), jnp.float32)
-        for block, part in enumerate((own_weights, next_weights)):
-            base = 192 * block + 64 * c
-            for k in range(4):
-                total = total + found[base : base + 64, 128 * k : 128 * k + 128] * part[k]
-        interpolated = jnp.sum(total, axis=0, keepdims=True)
-        wanted = target_velocity[c : c + 1] + time_step * contact_force[c : c + 1]
-        impulse[c : c + 1] = jnp.where(live, wanted - interpolated, 0.0)
-    near[10].start()
-    impulse_out[...] = impulse[...]
-    at_home = spread(impulse[...], own_weights, selector)
-    for number in (7, 8, 9):
-        near[number].wait_recv()
-    weights_from = spread_weights(
-        cells[256:512], weights_below[...], bricks_below[...], flags_below[...] == 2
-    )
-    selector_from = depth_cells(bricks_below[...])
-    near[10].wait_recv()
-    from_below = spread(impulse_below[...], weights_from, selector_from)
+    impulse = impulse_of(
+        star[192:576],
+        selector,
+        (own_weights, next_weights),
+        target_velocity[...] + time_step * contact_force[...],
+        flags,
+    )
+    impulse_out[...] = impulse
+    impulse_below = impulse_of(
+        star[0:384],
+        selector_below,
+        (below_weights, here_weights),
+        target_below[...] + time_step * contact_below[...],
+        flags_below,
+    )
+    at_home = spread(impulse, own_weights, selector)
+    from_below = spread(impulse_below, here_weights, selector_below)
     for c in range(3):
         for x in range(4):
             base = 64 * c + 16 * x
-            forced[c, x] = star[base : base + 16] + volume_ratio * (
+            forced[c, x] = star[192 + base : 208 + base] + volume_ratio * (
                 at_home[base : base + 16] + from_below[base : base + 16]
             )
 
@@ -403,9 +446,9 @@
     y_out[...] = table_times(rows, line_in[...])
     exchange_gx(s, t, y_out, x_in, own_sem.at[1], send_sem.at[1], recv_sem.at[1])
 
-    loads[4].wait()
-    loads[5].wait()
-    symbol = symbol_xz[...] + symbol_y[pl.ds(s, 1)]
+    for number in (4, 5, 13, 14):
+        loads[number].wait()
+    symbol = symbol_xz[...] + symbol_y[...]
     positive = symbol > 0
     factor = jnp.where(positive, -1.0 / jnp.where(positive, symbol, 1.0), 0.0)
     x_out[...] = table_times(columns_back, table_times(columns, x_in[...]) * factor)
@@ -452,7 +495,7 @@
 def step(velocity, owner_brick, particle_flags, weights, target_velocity, contact_force):
     tables = build_tables()
     inside = pl.BlockSpec(memory_space=pltpu.VMEM)
-    anywhere = pl.BlockSpec(memory_space=pl.ANY)
+    outside = pl.BlockSpec(memory_space=pltpu.HBM)
     f32, bf16 = jnp.float32, jnp.bfloat16
     return pl.pallas_call(
         step_kernel,
@@ -461,25 +504,30 @@
             jax.ShapeDtypeStruct((4, 16, 256), f32),
             jax.ShapeDtypeStruct((3, 128), f32),
         ),
-        in_specs=[anywhere, inside, inside, anywhere, inside, inside, inside]
-        + [anywhere] * 6
-        + [inside] * 2,
+        in_specs=[outside] * 15,
         out_specs=(inside, inside, inside),
         scratch_shapes=[
+            pltpu.VMEM((1, 128), jnp.int32),
+            pltpu.VMEM((1, 128), jnp.int32),
+            pltpu.VMEM((3, 128), f32),
+            pltpu.VMEM((3, 128), f32),
+            pltpu.VMEM((512, 128), bf16),
+            pltpu.VMEM((128, 128), f32),
+            pltpu.VMEM((1, 128), f32),
             pltpu.VMEM((2, 256, 256), bf16),
             pltpu.VMEM((2, 256, 256), bf16),
             pltpu.VMEM((2, 192, 256), bf16),
             pltpu.VMEM((2, 256, 192), bf16),
             pltpu.VMEM((2, 128, 192), bf16),
             pltpu.VMEM((2, 192, 128), bf16),
-            pltpu.VMEM((3, 10, 32, 256), f32),
+            pltpu.VMEM((3, 14, 32, 256), f32),
             pltpu.VMEM((128, 128), f32),
             pltpu.VMEM((128, 128), f32),
             pltpu.VMEM((1, 128), jnp.int32),
             pltpu.VMEM((1, 128), jnp.int32),
-            pltpu.VMEM((384, 256), f32),
             pltpu.VMEM((3, 128), f32),
             pltpu.VMEM((3, 128), f32),
+            pltpu.VMEM((576, 256), f32),
             pltpu.VMEM((3, 4, 16, 256), f32),
             pltpu.VMEM((2, 192, 128), f32),
             pltpu.VMEM((128, 256), f32),
@@ -491,15 +539,15 @@
             pltpu.VMEM((192, 128), f32),
             pltpu.VMEM((256, 128), f32),
             pltpu.VMEM((256, 128), f32),
-            pltpu.SemaphoreType.DMA((8,)),
-            pltpu.SemaphoreType.DMA((11,)),
-            pltpu.SemaphoreType.DMA((11,)),
+            pltpu.SemaphoreType.DMA((15,)),
+            pltpu.SemaphoreType.DMA((15,)),
+            pltpu.SemaphoreType.DMA((15,)),
             pltpu.SemaphoreType.DMA((4,)),
             pltpu.SemaphoreType.DMA((4,)),
             pltpu.SemaphoreType.DMA((4,)),
         ],
         compiler_params=pltpu.CompilerParams(
-            collective_id=0, has_side_effects=True, vmem_limit_bytes=32 * 1024 * 1024
+            collective_id=0, has_side_effects=True, vmem_limit_bytes=60 * 1024 * 1024
         ),
     )(
         velocity,

time: 67.1 us -> 56 us (0.83)
  local copies, waits for them, and re-layouts: 13.3 us -> 2.91 us
    unnamed x33 -> x7, local copies, waits for them, and re-layouts: 13.3 us -> 2.91 us
where the time goes in v2:
time: 56 us; the launch traced here: 55.9 us
  Pallas kernels  52.3 us (93%)
  local copies, waits for them, and re-layouts  2.91 us (5%)
  between operations  0.65 us (1%)
    pallas_call x1, Pallas kernels, step(): pl.pallas_call(step_kernel, out_shape=(jax.ShapeDtypeStruct((3, 4, 16, 25...  52.3 us
    unnamed x7, local copies, waits for them, and re-layouts  2.91 us

profile of v2, /device:TPU:1, one launch (start us, length us, event | category | flops | bytes accessed | tf_op | source)
XLA Modules:
  0.0 55.9 jit_solution(17510557860061427335)
XLA Ops:
  0.6 52.3 %shard_map.166 = (f32[3,4,16,256]{3,2,1,0:T(8,128)}, f32[4,16,256]{2,1,0:T(8,128)}, f32[3,128]{1,0:T(4,128)}) custom-call(f32[3,4,16,256]{3,2,1,0:T(8,128)} %velocity.1, s32[1,128]{1,0:T(1,128)} %bitcast.2, s32[1,128]{1,0:T(1,128)} %bitcast.3, f32[128,128]{1,0:T(8,128)} %weights_hbm.1, f32[3,128]{1,0:T(4,128)} %target_hbm.1, f32[3,128]{1,0:T(4,128)} %contact_hbm.1, ...), custom_call_target="tpu_custom_call" | custom-call | tf_op jit(solution)/shard_map/pallas_call | solution.py:500
  53.0 0.0 copy-start
  53.0 1.6 %copy.21 = f32[3,4,16,256]{3,2,1,0:T(8,128)} copy(f32[3,4,16,256]{3,2,1,0:T(8,128)} %get-tuple-element.6) | data formatting | bytes 393216
  54.6 0.0 copy-done
  54.6 0.0 copy-start.1
  54.6 0.6 %copy.22 = f32[4,16,256]{2,1,0:T(8,128)} copy(f32[4,16,256]{2,1,0:T(8,128)S(1)} %copy-done) | data formatting | bytes 131072
  55.3 0.0 copy-done.1
  55.3 0.6 %copy.23 = f32[3,128]{1,0:T(4,128)} copy(f32[3,128]{1,0:T(4,128)S(1)} %copy-done.1) | data formatting | bytes 3072
Async XLA Ops:
  53.0 1.7 %copy-start = (f32[4,16,256]{2,1,0:T(8,128)S(1)}, f32[4,16,256]{2,1,0:T(8,128)}, u32[]{:S(2)}) copy-start(f32[4,16,256]{2,1,0:T(8,128)} %get-tuple-element.7) | copy-start | bytes 196612
  54.6 0.7 %copy-start.1 = (f32[3,128]{1,0:T(4,128)S(1)}, f32[3,128]{1,0:T(4,128)}, u32[]{:S(2)}) copy-start(f32[3,128]{1,0:T(4,128)} %get-tuple-element.8) | copy-start | bytes 4612

commit v3 on v2

--- a/solution.py
+++ b/solution.py
@@ -219,15 +219,14 @@
     contact_hbm,
     cells_hbm,
     depth_hbm,
-    depth_back_hbm,
     rows_hbm,
     rows_back_hbm,
     columns_hbm,
     columns_back_hbm,
     symbol_xz_hbm,
     symbol_y_hbm,
-    velocity_new,
-    potential,
+    forced_out,
+    home_out,
     impulse_out,
     bricks,
     flags,
@@ -237,7 +236,6 @@
     symbol_xz,
     symbol_y,
     depth,
-    depth_back,
     rows,
     rows_back,
     columns,
@@ -250,6 +248,7 @@
     target_below,
     contact_below,
     star,
+    impulse_kept,
     forced,
     padded,
     classes,
@@ -267,6 +266,7 @@
     own_sem,
     send_sem,
     recv_sem,
+    save_sem,
 ):
     s = lax.axis_index("gx")
     t = lax.axis_index("gy")
@@ -277,7 +277,6 @@
         for number, (source, target) in enumerate(
             (
                 (depth_hbm, depth),
-                (depth_back_hbm, depth_back),
                 (rows_hbm.at[py], rows),
                 (rows_back_hbm.at[py], rows_back),
                 (columns_hbm.at[px], columns),
@@ -294,7 +293,7 @@
             )
         )
     ]
-    for number in (8, 9, 12, 7, 6, 10, 11, 0, 2, 4, 5, 13, 14, 3, 1):
+    for number in (7, 8, 11, 6, 5, 9, 10, 0, 1, 3, 4, 12, 13, 2):
         loads[number].start()
     line_in[...] = jnp.zeros_like(line_in)
     barrier = pltpu.get_barrier_semaphore()
@@ -353,7 +352,7 @@
     for copy in near:
         copy.start()
 
-    for number in (8, 9, 12, 7):
+    for number in (7, 8, 11, 6):
         loads[number].wait()
     own_weights, next_weights = both_weights(cells, weights, bricks, flags)
     selector = depth_cells(bricks[...])
@@ -361,7 +360,7 @@
         near[number].wait_recv()
     below_weights, here_weights = both_weights(cells, weights_below, bricks_below, flags_below)
     selector_below = depth_cells(bricks_below[...])
-    for number in (6, 10, 11):
+    for number in (5, 9, 10):
         loads[number].wait()
     for number in (0, 1, 2, 3, 4, 5, 6, 7, 10, 11, 13, 14):
         near[number].wait_recv()
@@ -387,7 +386,7 @@
         target_velocity[...] + time_step * contact_force[...],
         flags,
     )
-    impulse_out[...] = impulse
+    impulse_kept[...] = impulse
     impulse_below = impulse_of(
         star[0:384],
         selector_below,
@@ -403,6 +402,13 @@
             forced[c, x] = star[192 + base : 208 + base] + volume_ratio * (
                 at_home[base : base + 16] + from_below[base : base + 16]
             )
+
+    saved = [
+        pltpu.make_async_copy(impulse_kept, impulse_out, save_sem.at[0]),
+        pltpu.make_async_copy(forced, forced_out, save_sem.at[1]),
+    ]
+    for copy in saved:
+        copy.start()
 
     classes[...] = jnp.zeros_like(classes)
     row_number = lax.broadcasted_iota(jnp.int32, (16, 256), 0)
@@ -442,11 +448,11 @@
         ]
     exchange_gy(s, t, line_out, line_in, own_sem.at[0], send_sem.at[0], recv_sem.at[0])
 
-    loads[2].wait()
+    loads[1].wait()
     y_out[...] = table_times(rows, line_in[...])
     exchange_gx(s, t, y_out, x_in, own_sem.at[1], send_sem.at[1], recv_sem.at[1])
 
-    for number in (4, 5, 13, 14):
+    for number in (3, 4, 12, 13):
         loads[number].wait()
     symbol = symbol_xz[...] + symbol_y[...]
     positive = symbol > 0
@@ -454,10 +460,58 @@
     x_out[...] = table_times(columns_back, table_times(columns, x_in[...]) * factor)
     exchange_gx(s, t, x_out, y_in, own_sem.at[2], send_sem.at[2], recv_sem.at[2])
 
-    loads[3].wait()
+    loads[2].wait()
     line_back[...] = table_times(rows_back, y_in[...])
     exchange_gy(s, t, line_back, line_home, own_sem.at[3], send_sem.at[3], recv_sem.at[3])
 
+    saved.append(pltpu.make_async_copy(line_home, home_out, save_sem.at[2]))
+    saved[2].start()
+    for copy in saved:
+        copy.wait()
+    for copy in near:
+        copy.wait_send()
+
+
+def finish_kernel(
+    home_hbm,
+    depth_back_hbm,
+    forced_hbm,
+    impulse_hbm,
+    velocity_out,
+    potential_out,
+    impulse_out,
+    line_home,
+    depth_back,
+    forced,
+    classes,
+    padded,
+    potential,
+    velocity_new,
+    load_sem,
+    save_sem,
+):
+    loads = [
+        pltpu.make_async_copy(source, target, load_sem.at[number])
+        for number, (source, target) in enumerate(
+            ((home_hbm, line_home), (depth_back_hbm, depth_back), (forced_hbm, forced))
+        )
+    ]
+    for load in loads:
+        load.start()
+    saves = [
+        pltpu.make_async_copy(source, target, save_sem.at[number])
+        for number, (source, target) in enumerate(
+            (
+                (impulse_hbm, impulse_out),
+                (potential, potential_out),
+                (velocity_new.at[0], velocity_out.at[0]),
+                (velocity_new.at[1], velocity_out.at[1]),
+                (velocity_new.at[2], velocity_out.at[2]),
+            )
+        )
+    ]
+    saves[0].start()
+    loads[0].wait()
     loads[1].wait()
     home = jnp.concatenate(
         [
@@ -478,34 +532,43 @@
                 edge = place + (7 if b else 24)
                 put(padded, edge, 1, classes[base + 24 + xi : base + 25 + xi])
     for x in range(4):
+        potential[x] = take(padded, 32 * x + 40, 16)
+    saves[1].start()
+    loads[2].wait()
+    for x in range(4):
         base = 32 * (x + 1)
-        p = take(padded, base + 8, 16)
-        potential[x] = p
         velocity_new[0, x] = forced[0, x] - 0.5 * (
             take(padded, base + 40, 16) - take(padded, base - 24, 16)
         )
+    saves[2].start()
+    for x in range(4):
+        base = 32 * (x + 1)
         velocity_new[1, x] = forced[1, x] - 0.5 * (
             take(padded, base + 9, 16) - take(padded, base + 7, 16)
         )
+    saves[3].start()
+    for x in range(4):
+        p = potential[x]
         velocity_new[2, x] = forced[2, x] - 0.5 * (pltpu.roll(p, 255, 1) - pltpu.roll(p, 1, 1))
-    for copy in near:
-        copy.wait_send()
+    saves[4].start()
+    for save in saves:
+        save.wait()
 
 
 def step(velocity, owner_brick, particle_flags, weights, target_velocity, contact_force):
-    tables = build_tables()
-    inside = pl.BlockSpec(memory_space=pltpu.VMEM)
+    tables = list(build_tables())
     outside = pl.BlockSpec(memory_space=pltpu.HBM)
     f32, bf16 = jnp.float32, jnp.bfloat16
-    return pl.pallas_call(
+    depth_back = jnp.asarray(tables.pop(2))
+    forced, home, impulse = pl.pallas_call(
         step_kernel,
         out_shape=(
             jax.ShapeDtypeStruct((3, 4, 16, 256), f32),
-            jax.ShapeDtypeStruct((4, 16, 256), f32),
+            jax.ShapeDtypeStruct((256, 128), f32),
             jax.ShapeDtypeStruct((3, 128), f32),
         ),
-        in_specs=[outside] * 15,
-        out_specs=(inside, inside, inside),
+        in_specs=[outside] * 14,
+        out_specs=(outside, outside, outside),
         scratch_shapes=[
             pltpu.VMEM((1, 128), jnp.int32),
             pltpu.VMEM((1, 128), jnp.int32),
@@ -514,7 +577,6 @@
             pltpu.VMEM((512, 128), bf16),
             pltpu.VMEM((128, 128), f32),
             pltpu.VMEM((1, 128), f32),
-            pltpu.VMEM((2, 256, 256), bf16),
             pltpu.VMEM((2, 256, 256), bf16),
             pltpu.VMEM((2, 192, 256), bf16),
             pltpu.VMEM((2, 256, 192), bf16),
@@ -528,6 +590,7 @@
             pltpu.VMEM((3, 128), f32),
             pltpu.VMEM((3, 128), f32),
             pltpu.VMEM((576, 256), f32),
+            pltpu.VMEM((3, 128), f32),
             pltpu.VMEM((3, 4, 16, 256), f32),
             pltpu.VMEM((2, 192, 128), f32),
             pltpu.VMEM((128, 256), f32),
@@ -539,12 +602,13 @@
             pltpu.VMEM((192, 128), f32),
             pltpu.VMEM((256, 128), f32),
             pltpu.VMEM((256, 128), f32),
-            pltpu.SemaphoreType.DMA((15,)),
+            pltpu.SemaphoreType.DMA((14,)),
             pltpu.SemaphoreType.DMA((15,)),
             pltpu.SemaphoreType.DMA((15,)),
             pltpu.SemaphoreType.DMA((4,)),
             pltpu.SemaphoreType.DMA((4,)),
             pltpu.SemaphoreType.DMA((4,)),
+            pltpu.SemaphoreType.DMA((3,)),
         ],
         compiler_params=pltpu.CompilerParams(
             collective_id=0, has_side_effects=True, vmem_limit_bytes=60 * 1024 * 1024
@@ -558,6 +622,28 @@
         contact_force,
         *[jnp.asarray(table) for table in tables],
     )
+    return pl.pallas_call(
+        finish_kernel,
+        out_shape=(
+            jax.ShapeDtypeStruct((3, 4, 16, 256), f32),
+            jax.ShapeDtypeStruct((4, 16, 256), f32),
+            jax.ShapeDtypeStruct((3, 128), f32),
+        ),
+        in_specs=[outside] * 4,
+        out_specs=(outside, outside, outside),
+        scratch_shapes=[
+            pltpu.VMEM((256, 128), f32),
+            pltpu.VMEM((2, 256, 256), bf16),
+            pltpu.VMEM((3, 4, 16, 256), f32),
+            pltpu.VMEM((128, 256), f32),
+            pltpu.VMEM((2, 192, 128), f32),
+            pltpu.VMEM((4, 16, 256), f32),
+            pltpu.VMEM((3, 4, 16, 256), f32),
+            pltpu.SemaphoreType.DMA((3,)),
+            pltpu.SemaphoreType.DMA((5,)),
+        ],
+        compiler_params=pltpu.CompilerParams(vmem_limit_bytes=60 * 1024 * 1024),
+    )(home, depth_back, forced, impulse)
 
 
 def solution(mesh):

time: 56 us -> 54.7 us (0.977)
  local copies, waits for them, and re-layouts: 2.91 us -> 0 us
  Pallas kernels: 52.3 us -> 53.9 us
    unnamed x7 -> x0, local copies, waits for them, and re-layouts: 2.91 us -> none
    pallas_call x0 -> x1, Pallas kernels: none -> 2.06 us  [step(): pl.pallas_call(finish_kernel, out_shape=(jax.ShapeDtypeStruct((3, 4, 16,...]
where the time goes in v3:
time: 54.7 us; the launch traced here: 54.5 us
  Pallas kernels  53.9 us (99%)
  between operations  0.64 us (1%)
    pallas_call x1, Pallas kernels, step(): pl.pallas_call(step_kernel, out_shape=(jax.ShapeDtypeStruct((3, 4, 16, 25...  51.8 us
    pallas_call x1, Pallas kernels, step(): pl.pallas_call(finish_kernel, out_shape=(jax.ShapeDtypeStruct((3, 4, 16,...  2.06 us

profile of v3, /device:TPU:1, one launch (start us, length us, event | category | flops | bytes accessed | tf_op | source)
XLA Modules:
  0.0 54.5 jit_solution(7725007531020966591)
XLA Ops:
  0.6 51.8 %shard_map.166 = (f32[3,4,16,256]{3,2,1,0:T(8,128)}, f32[256,128]{1,0:T(8,128)}, f32[3,128]{1,0:T(4,128)}) custom-call(f32[3,4,16,256]{3,2,1,0:T(8,128)} %velocity.1, s32[1,128]{1,0:T(1,128)} %bitcast.2, s32[1,128]{1,0:T(1,128)} %bitcast.3, f32[128,128]{1,0:T(8,128)} %weights_hbm.1, f32[3,128]{1,0:T(4,128)} %target_hbm.1, f32[3,128]{1,0:T(4,128)} %contact_hbm.1, ...), custom_call_target="tpu_custom_call" | custom-call | tf_op jit(solution)/shard_map/pallas_call | solution.py:563
  52.5 2.1 %shard_map.167 = (f32[3,4,16,256]{3,2,1,0:T(8,128)}, f32[4,16,256]{2,1,0:T(8,128)}, f32[3,128]{1,0:T(4,128)}) custom-call(f32[256,128]{1,0:T(8,128)} %get-tuple-element.6.home_hbm, bf16[2,256,256]{2,1,0:T(8,128)(2,1)} %constant.18.clone.depth_back_hbm, f32[3,4,16,256]{3,2,1,0:T(8,128)} %get-tuple-element.7.forced_hbm, f32[3,128]{1,0:T(4,128)} %get-tuple-element.8.impulse_hbm), custom_call_target="tpu_custom_call" | custom-call | tf_op jit(solution)/shard_map/pallas_call | solution.py:625

commit v4 on v3

--- a/solution.py
+++ b/solution.py
@@ -156,24 +156,17 @@
     return [jnp.where(mask, found[64 * k : 64 * k + 64], 0.0) for k in range(4)]
 
 
-def both_weights(cells, weights, bricks, flags):
-    parts = ((cells[0:256], flags[...] > 0), (cells[256:512], flags[...] == 2))
-    return [spread_weights(part, weights[...], bricks[...], shown) for part, shown in parts]
-
-
-def impulse_of(star, selector, weights, wanted, flags):
+def part_of(star, selector, weights):
     top, rest = halves(star)
     found = dot(top, selector) + dot(rest, selector)
-    interpolated = []
+    sums = []
     for c in range(3):
         total = jnp.zeros((64, 128), jnp.float32)
-        for block in range(2):
-            base = 192 * block + 64 * c
-            for k in range(4):
-                cell = found[base : base + 64, 128 * k : 128 * k + 128]
-                total = total + cell * weights[block][k]
-        interpolated.append(jnp.sum(total, axis=0, keepdims=True))
-    return jnp.where(flags[...] > 0, wanted - jnp.concatenate(interpolated, axis=0), 0.0)
+        for k in range(4):
+            cell = found[64 * c : 64 * c + 64, 128 * k : 128 * k + 128]
+            total = total + cell * weights[k]
+        sums.append(jnp.sum(total, axis=0, keepdims=True))
+    return jnp.concatenate(sums, axis=0)
 
 
 def depth_cells(bricks):
@@ -245,8 +238,10 @@
     weights_below,
     bricks_below,
     flags_below,
-    target_below,
-    contact_below,
+    wanted,
+    wanted_below,
+    part_here,
+    part_next,
     star,
     impulse_kept,
     forced,
@@ -281,7 +276,7 @@
                 (rows_back_hbm.at[py], rows_back),
                 (columns_hbm.at[px], columns),
                 (columns_back_hbm.at[px], columns_back),
-                (velocity, region.at[:, pl.ds(5, 4), pl.ds(8, 16)]),
+                (velocity, region.at[:, pl.ds(1, 4), pl.ds(8, 16)]),
                 (weights_hbm, weights),
                 (bricks_hbm, bricks),
                 (flags_hbm, flags),
@@ -313,12 +308,9 @@
         )
         return carry
 
-    for dx in (-1, 1):
-        for dy in (-1, 1):
-            pl.semaphore_signal(barrier, inc=1, device_id=away(dx, dy), device_id_type=MESH)
     lax.fori_loop(1, GY, greet_gy, 0)
     lax.fori_loop(1, GX, greet_gx, 0)
-    pl.semaphore_wait(barrier, GX - 1 + GY - 1 + 4)
+    pl.semaphore_wait(barrier, GX - 1 + GY - 1)
 
     near = [
         pltpu.make_async_remote_copy(
@@ -331,41 +323,37 @@
         )
         for number, (source, target, where) in enumerate(
             (
-                (velocity.at[:, :, pl.ds(0, 1)], region.at[:, pl.ds(5, 4), pl.ds(24, 1)], (0, -1)),
-                (velocity.at[:, :, pl.ds(0, 1)], region.at[:, pl.ds(9, 4), pl.ds(24, 1)], (-1, -1)),
-                (velocity.at[:, :, pl.ds(0, 1)], region.at[:, pl.ds(1, 4), pl.ds(24, 1)], (1, -1)),
-                (velocity.at[:, :, pl.ds(15, 1)], region.at[:, pl.ds(5, 4), pl.ds(7, 1)], (0, 1)),
-                (velocity.at[:, :, pl.ds(15, 1)], region.at[:, pl.ds(9, 4), pl.ds(7, 1)], (-1, 1)),
-                (velocity.at[:, :, pl.ds(15, 1)], region.at[:, pl.ds(1, 4), pl.ds(7, 1)], (1, 1)),
-                (velocity.at[:, pl.ds(0, 1)], region.at[:, pl.ds(13, 1), pl.ds(8, 16)], (-2, 0)),
-                (velocity.at[:, pl.ds(3, 1)], region.at[:, pl.ds(0, 1), pl.ds(8, 16)], (2, 0)),
+                (velocity.at[:, :, pl.ds(0, 1)], region.at[:, pl.ds(1, 4), pl.ds(24, 1)], (0, -1)),
+                (velocity.at[:, :, pl.ds(15, 1)], region.at[:, pl.ds(1, 4), pl.ds(7, 1)], (0, 1)),
+                (velocity.at[:, pl.ds(0, 1)], region.at[:, pl.ds(5, 1), pl.ds(8, 16)], (-1, 0)),
+                (velocity.at[:, pl.ds(3, 1)], region.at[:, pl.ds(0, 1), pl.ds(8, 16)], (1, 0)),
                 (bricks_hbm, bricks_below, (1, 0)),
                 (flags_hbm, flags_below, (1, 0)),
-                (target_hbm, target_below, (1, 0)),
-                (contact_hbm, contact_below, (1, 0)),
                 (weights_hbm, weights_below, (1, 0)),
-                (velocity, region.at[:, pl.ds(9, 4), pl.ds(8, 16)], (-1, 0)),
-                (velocity, region.at[:, pl.ds(1, 4), pl.ds(8, 16)], (1, 0)),
+                (wanted, wanted_below, (1, 0)),
+                (part_here, part_next, (-1, 0)),
             )
         )
     ]
-    for copy in near:
-        copy.start()
+    for number in range(7):
+        near[number].start()
 
     for number in (7, 8, 11, 6):
         loads[number].wait()
-    own_weights, next_weights = both_weights(cells, weights, bricks, flags)
+    live = flags[...] > 0
+    own_weights = spread_weights(cells[0:256], weights[...], bricks[...], live)
     selector = depth_cells(bricks[...])
-    for number in (8, 9, 12):
+    for number in (4, 5, 6):
         near[number].wait_recv()
-    below_weights, here_weights = both_weights(cells, weights_below, bricks_below, flags_below)
+    here_weights = spread_weights(
+        cells[256:512], weights_below[...], bricks_below[...], flags_below[...] == 2
+    )
     selector_below = depth_cells(bricks_below[...])
     for number in (5, 9, 10):
         loads[number].wait()
-    for number in (0, 1, 2, 3, 4, 5, 6, 7, 10, 11, 13, 14):
+    for number in range(4):
         near[number].wait_recv()
-    for x in range(1, 13):
-        block, inner = (x - 1) // 4, (x - 1) % 4
+    for x in range(1, 5):
         centers = [region[c, x, 8:24] for c in range(3)]
         for c in range(3):
             v = centers[c]
@@ -376,30 +364,28 @@
             for d in range(3):
                 laplace = laplace + (uppers[d] + lowers[d])
                 carried = carried + centers[d] * (uppers[d] - lowers[d])
-            base = 192 * block + 64 * c + 16 * inner
+            base = 64 * c + 16 * (x - 1)
             star[base : base + 16] = v + time_step * (viscosity * laplace - 0.5 * carried)
 
-    impulse = impulse_of(
-        star[192:576],
-        selector,
-        (own_weights, next_weights),
-        target_velocity[...] + time_step * contact_force[...],
-        flags,
-    )
+    part_here[...] = part_of(star[...], selector_below, here_weights)
+    near[8].start()
+    wanted[...] = (
+        target_velocity[...]
+        + time_step * contact_force[...]
+        - part_of(star[...], selector, own_weights)
+    )
+    near[7].start()
+    near[7].wait_recv()
+    near[8].wait_recv()
+    impulse = jnp.where(live, wanted[...] - part_next[...], 0.0)
+    impulse_below = jnp.where(flags_below[...] > 0, wanted_below[...] - part_here[...], 0.0)
     impulse_kept[...] = impulse
-    impulse_below = impulse_of(
-        star[0:384],
-        selector_below,
-        (below_weights, here_weights),
-        target_below[...] + time_step * contact_below[...],
-        flags_below,
-    )
     at_home = spread(impulse, own_weights, selector)
     from_below = spread(impulse_below, here_weights, selector_below)
     for c in range(3):
         for x in range(4):
             base = 64 * c + 16 * x
-            forced[c, x] = star[192 + base : 208 + base] + volume_ratio * (
+            forced[c, x] = star[base : base + 16] + volume_ratio * (
                 at_home[base : base + 16] + from_below[base : base + 16]
             )
 
@@ -582,14 +568,16 @@
             pltpu.VMEM((2, 256, 192), bf16),
             pltpu.VMEM((2, 128, 192), bf16),
             pltpu.VMEM((2, 192, 128), bf16),
-            pltpu.VMEM((3, 14, 32, 256), f32),
+            pltpu.VMEM((3, 6, 32, 256), f32),
             pltpu.VMEM((128, 128), f32),
             pltpu.VMEM((128, 128), f32),
             pltpu.VMEM((1, 128), jnp.int32),
             pltpu.VMEM((1, 128), jnp.int32),
             pltpu.VMEM((3, 128), f32),
             pltpu.VMEM((3, 128), f32),
-            pltpu.VMEM((576, 256), f32),
+            pltpu.VMEM((3, 128), f32),
+            pltpu.VMEM((3, 128), f32),
+            pltpu.VMEM((192, 256), f32),
             pltpu.VMEM((3, 128), f32),
             pltpu.VMEM((3, 4, 16, 256), f32),
             pltpu.VMEM((2, 192, 128), f32),
@@ -603,8 +591,8 @@
             pltpu.VMEM((256, 128), f32),
             pltpu.VMEM((256, 128), f32),
             pltpu.SemaphoreType.DMA((14,)),
-            pltpu.SemaphoreType.DMA((15,)),
-            pltpu.SemaphoreType.DMA((15,)),
+            pltpu.SemaphoreType.DMA((9,)),
+            pltpu.SemaphoreType.DMA((9,)),
             pltpu.SemaphoreType.DMA((4,)),
             pltpu.SemaphoreType.DMA((4,)),
             pltpu.SemaphoreType.DMA((4,)),

time: 54.7 us -> 54 us (0.987)
  Pallas kernels: 53.9 us -> 53.2 us
    pallas_call x1, Pallas kernels: 51.8 us -> 51.1 us  [step(): pl.pallas_call(step_kernel, out_shape=(jax.ShapeDtypeStruct((3, 4, 16, 25...]
where the time goes in v4:
time: 54 us; the launch traced here: 53.8 us
  Pallas kernels  53.2 us (99%)
  between operations  0.64 us (1%)
    pallas_call x1, Pallas kernels, step(): pl.pallas_call(step_kernel, out_shape=(jax.ShapeDtypeStruct((3, 4, 16, 25...  51.1 us
    pallas_call x1, Pallas kernels, step(): pl.pallas_call(finish_kernel, out_shape=(jax.ShapeDtypeStruct((3, 4, 16,...  2.06 us

profile of v4, /device:TPU:1, one launch (start us, length us, event | category | flops | bytes accessed | tf_op | source)
XLA Modules:
  0.0 53.8 jit_solution(3706648328047767817)
XLA Ops:
  0.6 51.1 %shard_map.166 = (f32[3,4,16,256]{3,2,1,0:T(8,128)}, f32[256,128]{1,0:T(8,128)}, f32[3,128]{1,0:T(4,128)}) custom-call(f32[3,4,16,256]{3,2,1,0:T(8,128)} %velocity.1, s32[1,128]{1,0:T(1,128)} %bitcast.2, s32[1,128]{1,0:T(1,128)} %bitcast.3, f32[128,128]{1,0:T(8,128)} %weights_hbm.1, f32[3,128]{1,0:T(4,128)} %target_hbm.1, f32[3,128]{1,0:T(4,128)} %contact_hbm.1, ...), custom_call_target="tpu_custom_call" | custom-call | tf_op jit(solution)/shard_map/pallas_call | solution.py:549
  51.8 2.1 %shard_map.167 = (f32[3,4,16,256]{3,2,1,0:T(8,128)}, f32[4,16,256]{2,1,0:T(8,128)}, f32[3,128]{1,0:T(4,128)}) custom-call(f32[256,128]{1,0:T(8,128)} %get-tuple-element.6.home_hbm, bf16[2,256,256]{2,1,0:T(8,128)(2,1)} %constant.18.clone.depth_back_hbm, f32[3,4,16,256]{3,2,1,0:T(8,128)} %get-tuple-element.7.forced_hbm, f32[3,128]{1,0:T(4,128)} %get-tuple-element.8.impulse_hbm), custom_call_target="tpu_custom_call" | custom-call | tf_op jit(solution)/shard_map/pallas_call | solution.py:613

commit v5 on v4

--- a/solution.py
+++ b/solution.py
@@ -98,10 +98,12 @@
     own = pltpu.make_async_copy(source.at[pl.ds(3 * s, 3)], target.at[pl.ds(3 * s, 3)], own_sem)
     own.start()
 
-    def send(step, carry):
-        z = lax.rem(s // 8 + outward(step // 8, 8), 8)
-        x = lax.rem(lax.rem(s // 2, 4) + outward(lax.rem(step // 2, 4), 4), 4)
-        peer = 8 * z + 2 * x + lax.rem(s + 1 + step, 2)
+    chip = lax.rem(s // 2, 4)
+    beside = [
+        2 * lax.rem(chip + dx, 4) + lax.rem(s + dc, 2) for dx in (2, 1, 3, 0) for dc in (1, 0)
+    ]
+
+    def send_to(peer):
         pltpu.make_async_remote_copy(
             src_ref=source.at[pl.ds(3 * peer, 3)],
             dst_ref=target.at[pl.ds(3 * s, 3)],
@@ -110,9 +112,16 @@
             device_id=(peer, t),
             device_id_type=MESH,
         ).start()
+
+    def send(step, carry):
+        layer = 8 * lax.rem(s // 8 + outward(step, 8), 8)
+        for low in beside:
+            send_to(layer + low)
         return carry
 
-    lax.fori_loop(0, GX - 1, send, 0)
+    lax.fori_loop(0, 7, send, 0)
+    for low in beside[:7]:
+        send_to(8 * (s // 8) + low)
     own.wait()
     moved = pl.ds(0, 3 * (GX - 1))
     pltpu.make_async_copy(source.at[moved], target.at[moved], recv_sem).wait()
@@ -123,8 +132,8 @@
     own = pltpu.make_async_copy(source.at[pl.ds(32 * t, 32)], target.at[pl.ds(32 * t, 32)], own_sem)
     own.start()
 
-    def send(step, carry):
-        peer = lax.rem(t + outward(step, GY), GY)
+    for dy in (4, 3, 5, 2, 6, 1, 7):
+        peer = lax.rem(t + dy, GY)
         pltpu.make_async_remote_copy(
             src_ref=source.at[pl.ds(32 * peer, 27)],
             dst_ref=target.at[pl.ds(32 * t, 27)],
@@ -133,9 +142,6 @@
             device_id=(s, peer),
             device_id_type=MESH,
         ).start()
-        return carry
-
-    lax.fori_loop(0, GY - 1, send, 0)
     own.wait()
     moved = pl.ds(0, 27 * (GY - 1))
     pltpu.make_async_copy(source.at[moved], target.at[moved], recv_sem).wait()
@@ -296,20 +302,25 @@
     def away(dx, dy):
         return (lax.rem(s + GX + dx, GX), lax.rem(t + GY + dy, GY))
 
-    def greet_gx(step, carry):
-        pl.semaphore_signal(
-            barrier, inc=1, device_id=(lax.rem(s + step, GX), t), device_id_type=MESH
-        )
+    chip = lax.rem(s // 2, 4)
+    beside = [
+        2 * lax.rem(chip + dx, 4) + lax.rem(s + dc, 2) for dx in (2, 1, 3, 0) for dc in (1, 0)
+    ]
+
+    def greet(where):
+        pl.semaphore_signal(barrier, inc=1, device_id=where, device_id_type=MESH)
+
+    def greet_layer(step, carry):
+        layer = 8 * lax.rem(s // 8 + outward(step, 8), 8)
+        for low in beside:
+            greet((layer + low, t))
         return carry
 
-    def greet_gy(step, carry):
-        pl.semaphore_signal(
-            barrier, inc=1, device_id=(s, lax.rem(t + step, GY)), device_id_type=MESH
-        )
-        return carry
-
-    lax.fori_loop(1, GY, greet_gy, 0)
-    lax.fori_loop(1, GX, greet_gx, 0)
+    lax.fori_loop(0, 7, greet_layer, 0)
+    for low in beside[:7]:
+        greet((8 * (s // 8) + low, t))
+    for dy in (4, 3, 5, 2, 6, 1, 7):
+        greet((s, lax.rem(t + dy, GY)))
     pl.semaphore_wait(barrier, GX - 1 + GY - 1)
 
     near = [

time: 54 us -> 52.1 us (0.965)
  Pallas kernels: 53.2 us -> 51.3 us
    pallas_call x1, Pallas kernels: 51.1 us -> 49.3 us  [step(): pl.pallas_call(step_kernel, out_shape=(jax.ShapeDtypeStruct((3, 4, 16, 25...]
where the time goes in v5:
time: 52.1 us; the launch traced here: 52 us
  Pallas kernels  51.3 us (98%)
  between operations  0.64 us (1%)
    pallas_call x1, Pallas kernels, step(): pl.pallas_call(step_kernel, out_shape=(jax.ShapeDtypeStruct((3, 4, 16, 25...  49.3 us
    pallas_call x1, Pallas kernels, step(): pl.pallas_call(finish_kernel, out_shape=(jax.ShapeDtypeStruct((3, 4, 16,...  2.06 us

profile of v5, /device:TPU:1, one launch (start us, length us, event | category | flops | bytes accessed | tf_op | source)
XLA Modules:
  0.0 52.0 jit_solution(13936613050740646142)
XLA Ops:
  0.6 49.3 %shard_map.166 = (f32[3,4,16,256]{3,2,1,0:T(8,128)}, f32[256,128]{1,0:T(8,128)}, f32[3,128]{1,0:T(4,128)}) custom-call(f32[3,4,16,256]{3,2,1,0:T(8,128)} %velocity.1, s32[1,128]{1,0:T(1,128)} %bitcast.2, s32[1,128]{1,0:T(1,128)} %bitcast.3, f32[128,128]{1,0:T(8,128)} %weights_hbm.1, f32[3,128]{1,0:T(4,128)} %target_hbm.1, f32[3,128]{1,0:T(4,128)} %contact_hbm.1, ...), custom_call_target="tpu_custom_call" | custom-call | tf_op jit(solution)/shard_map/pallas_call | solution.py:560
  49.9 2.1 %shard_map.167 = (f32[3,4,16,256]{3,2,1,0:T(8,128)}, f32[4,16,256]{2,1,0:T(8,128)}, f32[3,128]{1,0:T(4,128)}) custom-call(f32[256,128]{1,0:T(8,128)} %get-tuple-element.6.home_hbm, bf16[2,256,256]{2,1,0:T(8,128)(2,1)} %constant.18.clone.depth_back_hbm, f32[3,4,16,256]{3,2,1,0:T(8,128)} %get-tuple-element.7.forced_hbm, f32[3,128]{1,0:T(4,128)} %get-tuple-element.8.impulse_hbm), custom_call_target="tpu_custom_call" | custom-call | tf_op jit(solution)/shard_map/pallas_call | solution.py:624

commit v6 on v5

--- a/solution.py
+++ b/solution.py
@@ -113,15 +113,11 @@
             device_id_type=MESH,
         ).start()
 
-    def send(step, carry):
-        layer = 8 * lax.rem(s // 8 + outward(step, 8), 8)
-        for low in beside:
-            send_to(layer + low)
-        return carry
-
-    lax.fori_loop(0, 7, send, 0)
-    for low in beside[:7]:
-        send_to(8 * (s // 8) + low)
+    layers = [8 * lax.rem(s // 8 + dz, 8) for dz in range(8)]
+    hops = [2, 2, 1, 1, 1, 1, 0, 0]
+    order = [(dz, low) for dz in range(8) for low in range(8) if dz or low < 7]
+    for dz, low in sorted(order, key=lambda to: -min(to[0], 8 - to[0]) - hops[to[1]]):
+        send_to(layers[dz] + beside[low])
     own.wait()
     moved = pl.ds(0, 3 * (GX - 1))
     pltpu.make_async_copy(source.at[moved], target.at[moved], recv_sem).wait()

time: 52.1 us -> 51.8 us (level)
  no operation moved by 1% of the time
where the time goes in v6:
time: 51.8 us; the launch traced here: 51.7 us
  Pallas kernels  51 us (98%)
  between operations  0.64 us (1%)
    pallas_call x1, Pallas kernels, step(): pl.pallas_call(step_kernel, out_shape=(jax.ShapeDtypeStruct((3, 4, 16, 25...  49 us
    pallas_call x1, Pallas kernels, step(): pl.pallas_call(finish_kernel, out_shape=(jax.ShapeDtypeStruct((3, 4, 16,...  2.06 us

profile of v6, /device:TPU:1, one launch (start us, length us, event | category | flops | bytes accessed | tf_op | source)
XLA Modules:
  0.0 51.7 jit_solution(9096991628825639158)
XLA Ops:
  0.6 49.0 %shard_map.166 = (f32[3,4,16,256]{3,2,1,0:T(8,128)}, f32[256,128]{1,0:T(8,128)}, f32[3,128]{1,0:T(4,128)}) custom-call(f32[3,4,16,256]{3,2,1,0:T(8,128)} %velocity.1, s32[1,128]{1,0:T(1,128)} %bitcast.2, s32[1,128]{1,0:T(1,128)} %bitcast.3, f32[128,128]{1,0:T(8,128)} %weights_hbm.1, f32[3,128]{1,0:T(4,128)} %target_hbm.1, f32[3,128]{1,0:T(4,128)} %contact_hbm.1, ...), custom_call_target="tpu_custom_call" | custom-call | tf_op jit(solution)/shard_map/pallas_call | solution.py:556
  49.6 2.1 %shard_map.167 = (f32[3,4,16,256]{3,2,1,0:T(8,128)}, f32[4,16,256]{2,1,0:T(8,128)}, f32[3,128]{1,0:T(4,128)}) custom-call(f32[256,128]{1,0:T(8,128)} %get-tuple-element.6.home_hbm, bf16[2,256,256]{2,1,0:T(8,128)(2,1)} %constant.18.clone.depth_back_hbm, f32[3,4,16,256]{3,2,1,0:T(8,128)} %get-tuple-element.7.forced_hbm, f32[3,128]{1,0:T(4,128)} %get-tuple-element.8.impulse_hbm), custom_call_target="tpu_custom_call" | custom-call | tf_op jit(solution)/shard_map/pallas_call | solution.py:620
